TPU v7x, 512 devices: a whole 4x8x8 slice. The times are simulated.
512 devices in a mesh: dp: 4 (over y_lo), seq: 16 (over z, y_hi), head: 8 (over x, core).
Axes of the slice: x: 4, y: 8 (y_hi: 2, y_lo: 4; y = y_hi * 4 + y_lo), z: 8, core: 2. Of those that a mesh axis runs over, the one named last changes fastest.
Arguments:
- spatial_query: bfloat16 [4, 16, 256, 2048], P('dp', 'seq', None, 'head'), may hold values from -10 to 10
- spatial_key: bfloat16 [4, 16, 256, 2048], P('dp', 'seq', None, 'head'), may hold values from -10 to 10
- spatial_value: bfloat16 [4, 16, 256, 2048], P('dp', 'seq', None, 'head'), may hold values from -6 to 6
- spatial_mask: int32 [4, 16, 16, 2, 2], P('dp', 'seq', 'head'), may hold values from 0 to 1, as said below
- temporal_query: bfloat16 [4, 16, 256, 2048], P('dp', 'seq', None, 'head'), may hold values from -10 to 10
- temporal_key: bfloat16 [4, 16, 256, 2048], P('dp', 'seq', None, 'head'), may hold values from -10 to 10
- temporal_value: bfloat16 [4, 16, 256, 2048], P('dp', 'seq', None, 'head'), may hold values from -6 to 6
- spatial_proj: bfloat16 [2048, 3072], P('head', 'seq'), may hold values from -0.125 to 0.125
- temporal_proj: bfloat16 [2048, 3072], P('head', 'seq'), may hold values from -0.125 to 0.125
- cotangent: bfloat16 [4, 16, 256, 3072], P('dp', 'seq', None, 'head'), may hold values from -6 to 6
Outputs:
- block_update: bfloat16 [4, 16, 256, 3072], P('dp', 'seq', None, 'head')
- grad_spatial_query: bfloat16 [4, 16, 256, 2048], P('dp', 'seq', None, 'head')
- grad_spatial_key: bfloat16 [4, 16, 256, 2048], P('dp', 'seq', None, 'head')
- grad_spatial_value: bfloat16 [4, 16, 256, 2048], P('dp', 'seq', None, 'head')
- grad_temporal_query: bfloat16 [4, 16, 256, 2048], P('dp', 'seq', None, 'head')
- grad_temporal_key: bfloat16 [4, 16, 256, 2048], P('dp', 'seq', None, 'head')
- grad_temporal_value: bfloat16 [4, 16, 256, 2048], P('dp', 'seq', None, 'head')
- grad_spatial_proj: float32 [2048, 3072], P('head', 'seq')
- grad_temporal_proj: float32 [2048, 3072], P('head', 'seq')
Inputs may be any that keep to these rules, and one draw needn't show every extreme that they name: `spatial_mask`: every tile on the diagonal (a query tile with its own key tile) is 1.
All inputs are finite; a program needn't handle non-finite values.
Results may differ from a plain program's by a relative error of at most 0.019.
Values may be sent and summed in bfloat16 or wider, within the bound.
A program may use at most 64 MiB of HBM per device.

v0:
```python
import math

import jax
import jax.numpy as jnp
from jax import lax
from jax.sharding import PartitionSpec as P


def spatial_forward(query, keys, values, mask, score_scale):
    clip_count, frame_count, tokens, head_count, head_dim = query.shape
    blocks = mask.shape[-1]
    tile_size = tokens // blocks
    scores = (
        jnp.einsum("cfqhd,cfkhd->cfhqk", query, keys, preferred_element_type=jnp.float32)
        * score_scale
    )
    scores = scores.reshape(
        clip_count, frame_count, head_count, blocks, tile_size, blocks, tile_size
    )
    allowed = mask[:, :, :, :, None, :, None] > 0
    scores = jnp.where(allowed, scores, -jnp.inf).reshape(
        clip_count, frame_count, head_count, tokens, tokens
    )
    shares = jax.nn.softmax(scores, axis=-1)
    weights = shares.astype(jnp.bfloat16)
    attended = jnp.einsum(
        "cfhqk,cfkhd->cfqhd", weights, values, preferred_element_type=jnp.float32
    ).astype(jnp.bfloat16)
    return (shares, weights, attended)


def spatial_backward(query, keys, values, shares, weights, grad_att, score_scale):
    grad_shares = jnp.einsum(
        "cfqhd,cfkhd->cfhqk", grad_att, values, preferred_element_type=jnp.float32
    )
    centre = jnp.sum(shares * grad_shares, axis=-1, keepdims=True)
    grad_scores = (shares * (grad_shares - centre)).astype(jnp.bfloat16)
    grad_query = (
        jnp.einsum("cfhqk,cfkhd->cfqhd", grad_scores, keys, preferred_element_type=jnp.float32)
        * score_scale
    ).astype(jnp.bfloat16)
    grad_keys = (
        jnp.einsum("cfhqk,cfqhd->cfkhd", grad_scores, query, preferred_element_type=jnp.float32)
        * score_scale
    ).astype(jnp.bfloat16)
    grad_values = jnp.einsum(
        "cfhqk,cfqhd->cfkhd", weights, grad_att, preferred_element_type=jnp.float32
    ).astype(jnp.bfloat16)
    return (grad_query, grad_keys, grad_values)


def temporal_forward(query, keys, values, score_scale):
    scores = (
        jnp.einsum("cfthd,cgthd->cthfg", query, keys, preferred_element_type=jnp.float32)
        * score_scale
    )
    shares = jax.nn.softmax(scores, axis=-1)
    weights = shares.astype(jnp.bfloat16)
    attended = jnp.einsum(
        "cthfg,cgthd->cfthd", weights, values, preferred_element_type=jnp.float32
    ).astype(jnp.bfloat16)
    return (shares, weights, attended)


def temporal_backward(query, keys, values, shares, weights, grad_att, score_scale):
    grad_shares = jnp.einsum(
        "cfthd,cgthd->cthfg", grad_att, values, preferred_element_type=jnp.float32
    )
    centre = jnp.sum(shares * grad_shares, axis=-1, keepdims=True)
    grad_scores = (shares * (grad_shares - centre)).astype(jnp.bfloat16)
    grad_query = (
        jnp.einsum("cthfg,cgthd->cfthd", grad_scores, keys, preferred_element_type=jnp.float32)
        * score_scale
    ).astype(jnp.bfloat16)
    grad_keys = (
        jnp.einsum("cthfg,cfthd->cgthd", grad_scores, query, preferred_element_type=jnp.float32)
        * score_scale
    ).astype(jnp.bfloat16)
    grad_values = jnp.einsum(
        "cthfg,cfthd->cgthd", weights, grad_att, preferred_element_type=jnp.float32
    ).astype(jnp.bfloat16)
    return (grad_query, grad_keys, grad_values)


def per_device(
    spatial_query,
    spatial_key,
    spatial_value,
    spatial_mask,
    temporal_query,
    temporal_key,
    temporal_value,
    spatial_proj,
    temporal_proj,
    cotangent,
):
    clip_count, frame_count, token_count, local_width = spatial_query.shape
    head_count = spatial_mask.shape[2]
    head_dim = local_width // head_count
    score_scale = 1.0 / math.sqrt(head_dim)
    row_count = clip_count * frame_count * token_count
    split_shape = (clip_count, frame_count, token_count, head_count, head_dim)
    frame_layout = (clip_count, frame_count, token_count, local_width)
    s_query = spatial_query.reshape(split_shape)
    s_key = spatial_key.reshape(split_shape)
    s_value = spatial_value.reshape(split_shape)
    s_shares, s_weights, s_attended = spatial_forward(
        s_query, s_key, s_value, spatial_mask, score_scale
    )
    regrouped = (
        lax.all_to_all(temporal_query, "seq", split_axis=2, concat_axis=1, tiled=True),
        lax.all_to_all(temporal_key, "seq", split_axis=2, concat_axis=1, tiled=True),
        lax.all_to_all(temporal_value, "seq", split_axis=2, concat_axis=1, tiled=True),
    )
    token_layout = regrouped[0].shape
    token_split = token_layout[:3] + (head_count, head_dim)
    t_query = regrouped[0].reshape(token_split)
    t_key = regrouped[1].reshape(token_split)
    t_value = regrouped[2].reshape(token_split)
    t_shares, t_weights, t_attended_tok = temporal_forward(t_query, t_key, t_value, score_scale)
    t_attended = lax.all_to_all(
        t_attended_tok.reshape(token_layout), "seq", split_axis=1, concat_axis=2, tiled=True
    )
    spatial_rows = s_attended.reshape(row_count, local_width)
    temporal_rows = t_attended.reshape(row_count, local_width)
    stacked = jnp.stack((spatial_proj, temporal_proj))
    piece = lax.all_gather(stacked, "seq", axis=2, tiled=True)
    result = jnp.dot(spatial_rows, piece[0], preferred_element_type=jnp.float32)
    partial_value = result + jnp.dot(temporal_rows, piece[1], preferred_element_type=jnp.float32)
    summed = lax.psum_scatter(
        partial_value.astype(jnp.bfloat16), "head", scatter_dimension=1, tiled=True
    ).astype(jnp.float32)
    block_update = summed.astype(jnp.bfloat16).reshape(
        clip_count, frame_count, token_count, summed.shape[1]
    )
    cot_full = lax.all_gather(cotangent, "head", axis=3, tiled=True)
    width = cot_full.shape[3]
    cot_rows = cot_full.reshape(row_count, width)
    contract = (((1,), (1,)), ((), ()))
    piece = lax.all_gather(stacked, "seq", axis=2, tiled=True)
    first = lax.dot_general(cot_rows, piece[0], contract, preferred_element_type=jnp.float32)
    second = lax.dot_general(cot_rows, piece[1], contract, preferred_element_type=jnp.float32)
    grad_spatial_rows = first
    grad_temporal_rows = second
    grad_s_att = grad_spatial_rows.astype(jnp.bfloat16).reshape(split_shape)
    grad_t_att = grad_temporal_rows.astype(jnp.bfloat16).reshape(frame_layout)
    cot_columns = lax.all_to_all(cot_full, "seq", split_axis=3, concat_axis=1, tiled=True)
    spatial_att4 = s_attended.reshape(frame_layout)
    first = jnp.einsum(
        "cftk,cftd->kd",
        lax.all_gather(spatial_att4, "seq", axis=1, tiled=True),
        cot_columns,
        preferred_element_type=jnp.float32,
    )
    second = jnp.einsum(
        "cftk,cftd->kd",
        lax.all_gather(t_attended, "seq", axis=1, tiled=True),
        cot_columns,
        preferred_element_type=jnp.float32,
    )
    replica_totals = (
        lax.psum(first.astype(jnp.bfloat16), "dp").astype(jnp.float32),
        lax.psum(second.astype(jnp.bfloat16), "dp").astype(jnp.float32),
    )
    replicas = lax.axis_size("dp")
    grad_spatial_proj = replica_totals[0] / replicas
    grad_temporal_proj = replica_totals[1] / replicas
    sq_grad, sk_grad, sv_grad = spatial_backward(
        s_query, s_key, s_value, s_shares, s_weights, grad_s_att, score_scale
    )
    grad_t_tok = lax.all_to_all(grad_t_att, "seq", split_axis=2, concat_axis=1, tiled=True).reshape(
        token_split
    )
    tq_grad, tk_grad, tv_grad = temporal_backward(
        t_query, t_key, t_value, t_shares, t_weights, grad_t_tok, score_scale
    )
    returned = (
        lax.all_to_all(
            tq_grad.reshape(token_layout), "seq", split_axis=1, concat_axis=2, tiled=True
        ),
        lax.all_to_all(
            tk_grad.reshape(token_layout), "seq", split_axis=1, concat_axis=2, tiled=True
        ),
        lax.all_to_all(
            tv_grad.reshape(token_layout), "seq", split_axis=1, concat_axis=2, tiled=True
        ),
    )
    return (
        block_update,
        sq_grad.reshape(frame_layout),
        sk_grad.reshape(frame_layout),
        sv_grad.reshape(frame_layout),
        returned[0],
        returned[1],
        returned[2],
        grad_spatial_proj,
        grad_temporal_proj,
    )


def solution(mesh):
    placed = (
        P("dp", "seq", None, "head"),
        P("dp", "seq", None, "head"),
        P("dp", "seq", None, "head"),
        P("dp", "seq", "head", None, None),
        P("dp", "seq", None, "head"),
        P("dp", "seq", None, "head"),
        P("dp", "seq", None, "head"),
        P("head", "seq"),
        P("head", "seq"),
        P("dp", "seq", None, "head"),
    )
    return jax.shard_map(
        per_device,
        mesh=mesh,
        in_specs=placed,
        out_specs=(
            P("dp", "seq", None, "head"),
            P("dp", "seq", None, "head"),
            P("dp", "seq", None, "head"),
            P("dp", "seq", None, "head"),
            P("dp", "seq", None, "head"),
            P("dp", "seq", None, "head"),
            P("dp", "seq", None, "head"),
            P("head", "seq"),
            P("head", "seq"),
        ),
        check_vma=False,
    )
```

profile of v0, /device:TPU:56, one launch (start us, length us, event | category | flops | bytes accessed | tf_op | source)
XLA Modules:
  0.0 538.6 jit_solution(4427235979630035277)
XLA Ops:
  7.9 1.1 copy.207
  9.6 1.4 reduce.21
  11.7 15.7 %all-to-all-start = ((bf16[16,2,2048]{2,1,0:T(2,128)(2,1)}), bf16[16,2,2048]{2,1,0:T(2,128)(2,1)S(1)}, u32[]{:S(2)}, u32[]{:S(2)}) async-start(bf16[16,2,2048]{2,1,0:T(2,128)(2,1)} %reshape.314), calls=%async_computation | async-start | bytes 262144 | tf_op jit(solution)/shard_map/all_to_all | solution.py:111
  27.6 1.4 reduce.20
  29.7 6.2 %all-to-all-done = bf16[16,2,2048]{2,1,0:T(2,128)(2,1)S(1)} async-done(((bf16[16,2,2048]{2,1,0:T(2,128)(2,1)}), bf16[16,2,2048]{2,1,0:T(2,128)(2,1)S(1)}, u32[]{:S(2)}, u32[]{:S(2)}) %all-to-all-start) | async-done | bytes 131104 | tf_op jit(solution)/shard_map/all_to_all | solution.py:111
  35.9 8.0 %all-to-all-start.1 = ((bf16[16,2,2048]{2,1,0:T(2,128)(2,1)}), bf16[16,2,2048]{2,1,0:T(2,128)(2,1)S(1)}, u32[]{:S(2)}, u32[]{:S(2)}) async-start(bf16[16,2,2048]{2,1,0:T(2,128)(2,1)} %reshape.312), calls=%async_computation.1 | async-start | bytes 262144 | tf_op jit(solution)/shard_map/all_to_all | solution.py:112
  44.1 1.4 reduce.19
  46.3 5.9 %all-to-all-done.1 = bf16[16,2,2048]{2,1,0:T(2,128)(2,1)S(1)} async-done(((bf16[16,2,2048]{2,1,0:T(2,128)(2,1)}), bf16[16,2,2048]{2,1,0:T(2,128)(2,1)S(1)}, u32[]{:S(2)}, u32[]{:S(2)}) %all-to-all-start.1) | async-done | bytes 131104 | tf_op jit(solution)/shard_map/all_to_all | solution.py:112
  52.2 8.2 %all-to-all-start.2 = ((bf16[16,2,2048]{2,1,0:T(2,128)(2,1)}), bf16[16,2,2048]{2,1,0:T(2,128)(2,1)S(1)}, u32[]{:S(2)}, u32[]{:S(2)}) async-start(bf16[16,2,2048]{2,1,0:T(2,128)(2,1)} %reshape.310), calls=%async_computation.2 | async-start | bytes 262144 | tf_op jit(solution)/shard_map/all_to_all | solution.py:113
  62.1 6.7 %all-to-all-done.2 = bf16[16,2,2048]{2,1,0:T(2,128)(2,1)S(1)} async-done(((bf16[16,2,2048]{2,1,0:T(2,128)(2,1)}), bf16[16,2,2048]{2,1,0:T(2,128)(2,1)S(1)}, u32[]{:S(2)}, u32[]{:S(2)}) %all-to-all-start.2) | async-done | bytes 131104 | tf_op jit(solution)/shard_map/all_to_all | solution.py:113
  71.3 16.2 %all_to_all.99 = bf16[1,16,16,256]{3,2,0,1:T(8,128)(2,1)} all-to-all(bf16[1,16,16,256]{3,2,0,1:T(8,128)(2,1)S(1)} %bitcast.185), channel_id=1, replica_groups=mesh['dp'=4,'seq'=16,'head'=8] {'seq'}, dimensions={1} | all-to-all | bytes 262144 | tf_op jit(solution)/shard_map/all_to_all | solution.py:121
  88.8 1.2 fusion.75
  90.6 0.8 copy.146
  92.4 7.7 %copy.147 = bf16[1,1,256,3072]{2,1,0,3:T(2,128)(2,1)S(1)} copy(bf16[1,1,256,3072]{3,2,1,0:T(8,128)(2,1)} %all-gather.7.cloned.1.call-done) | data formatting | bytes 3145728 | tf_op jit(solution)/shard_map/all_gather | solution.py:136
  100.1 16.7 %reduce.23 = bf16[3072,256]{1,0:T(8,128)(2,1)} reduce(bf16[3072,1,1,256]{3,2,1,0:T(2,128)(2,1)S(1)} %bitcast.170, bf16[]{:T(256)} %broadcast.106), dimensions={1,2}, to_apply=%bitcast.139.reduce_sub_computation | reduce | bytes 3145730
  116.8 3.7 reshape.318
  120.5 43.4 %all_to_all.100 = bf16[16,2,24576]{2,1,0:T(2,128)(2,1)} all-to-all(bf16[16,2,24576]{2,1,0:T(2,128)(2,1)S(1)} %reshape.318), channel_id=1, replica_groups=mesh['dp'=4,'seq'=16,'head'=8] {'seq'}, dimensions={0} | all-to-all | bytes 3145728 | tf_op jit(solution)/shard_map/all_to_all | solution.py:147
  164.0 8.1 %reshape.319 = bf16[3072,1,1,256]{3,2,1,0:T(2,128)(2,1)S(1)} reshape(bf16[16,2,24576]{2,1,0:T(2,128)(2,1)} %all_to_all.100) | data formatting | bytes 3145728
  172.1 1.4 copy.161
  173.5 39.9 %all-gather.11.cloned.1.call-done = bf16[1,16,256,256]{3,2,0,1:T(8,128)(2,1)} async-done(((bf16[1,1,256,256]{3,2,0,1:T(8,128)(2,1)}), bf16[1,16,256,256]{3,2,0,1:T(8,128)(2,1)}) %all-gather.11.cloned.1.call-update) | async-done | bytes 2097168 | tf_op jit(solution)/shard_map/all_gather | solution.py:157
  213.4 3.4 fusion.33
  216.8 95.1 %all-gather.9.cloned.1.call-done = bf16[1,16,256,256]{3,2,0,1:T(8,128)(2,1)} async-done(((bf16[1,1,256,256]{3,2,0,1:T(8,128)(2,1)}), bf16[1,16,256,256]{3,2,0,1:T(8,128)(2,1)}) %all-gather.9.cloned.1.call-update) | async-done | bytes 2097168 | tf_op jit(solution)/shard_map/all_gather | solution.py:151
  311.9 2.8 fusion.36
  314.8 112.8 %all-gather.5.cloned.1.call-done = bf16[2,256,3072]{1,2,0:T(8,128)(2,1)} async-done(((bf16[2,256,192]{1,2,0:T(8,128)(2,1)}), bf16[2,256,3072]{1,2,0:T(8,128)(2,1)}) %all-gather.5.cloned.1.call-update) | async-done | bytes 3145744 | tf_op jit(solution)/shard_map/all_gather | solution.py:127
  427.6 2.2 fusion.11
  430.6 1.6 copy.159
  432.2 3.3 fusion.39
  435.5 1.1 copy.133
  436.6 2.0 reduce.22
  438.6 1.6 reshape.316
  440.2 9.3 %all-to-all-start.4 = ((bf16[16,2,2048]{2,1,0:T(2,128)(2,1)}), bf16[16,2,2048]{2,1,0:T(2,128)(2,1)S(1)}, u32[]{:S(2)}, u32[]{:S(2)}) async-start(bf16[16,2,2048]{2,1,0:T(2,128)(2,1)} %reshape.316), calls=%async_computation.4 | async-start | bytes 262144 | tf_op jit(solution)/shard_map/all_to_all | solution.py:171
  449.6 2.1 fusion.21
  452.4 5.3 all-to-all-done.4
  459.4 0.7 reshape.296
  460.1 8.2 %all-to-all-start.6 = ((bf16[1,16,16,256]{3,2,0,1:T(8,128)(2,1)}), bf16[1,16,16,256]{3,2,0,1:T(8,128)(2,1)S(1)}, u32[]{:S(2)}, u32[]{:S(2)}) async-start(bf16[1,16,16,256]{3,2,0,1:T(8,128)(2,1)} %bitcast.40), calls=%async_computation.6 | async-start | bytes 262144 | tf_op jit(solution)/shard_map/all_to_all | solution.py:181
  468.8 0.7 reshape.295
  469.6 7.2 %all-to-all-done.6 = bf16[1,16,16,256]{3,2,0,1:T(8,128)(2,1)S(1)} async-done(((bf16[1,16,16,256]{3,2,0,1:T(8,128)(2,1)}), bf16[1,16,16,256]{3,2,0,1:T(8,128)(2,1)S(1)}, u32[]{:S(2)}, u32[]{:S(2)}) %all-to-all-start.6) | async-done | bytes 131104 | tf_op jit(solution)/shard_map/all_to_all | solution.py:181
  476.7 8.1 %all-to-all-start.5 = ((bf16[1,16,16,256]{3,2,0,1:T(8,128)(2,1)}), bf16[1,16,16,256]{3,2,0,1:T(8,128)(2,1)S(1)}, u32[]{:S(2)}, u32[]{:S(2)}) async-start(bf16[1,16,16,256]{3,2,0,1:T(8,128)(2,1)} %bitcast.35), calls=%async_computation.5 | async-start | bytes 262144 | tf_op jit(solution)/shard_map/all_to_all | solution.py:178
  485.4 0.7 reshape.297
  486.1 7.2 %all-to-all-done.5 = bf16[1,16,16,256]{3,2,0,1:T(8,128)(2,1)S(1)} async-done(((bf16[1,16,16,256]{3,2,0,1:T(8,128)(2,1)}), bf16[1,16,16,256]{3,2,0,1:T(8,128)(2,1)S(1)}, u32[]{:S(2)}, u32[]{:S(2)}) %all-to-all-start.5) | async-done | bytes 131104 | tf_op jit(solution)/shard_map/all_to_all | solution.py:178
  493.3 8.0 %all-to-all-start.7 = ((bf16[1,16,16,256]{3,2,0,1:T(8,128)(2,1)}), bf16[1,16,16,256]{3,2,0,1:T(8,128)(2,1)S(1)}, u32[]{:S(2)}, u32[]{:S(2)}) async-start(bf16[1,16,16,256]{3,2,0,1:T(8,128)(2,1)} %bitcast.44), calls=%async_computation.7 | async-start | bytes 262144 | tf_op jit(solution)/shard_map/all_to_all | solution.py:184
  501.9 0.8 copy.149
  502.7 0.8 copy.150
  503.4 0.8 copy.151
  504.2 1.7 convert_multiply_fusion
  505.9 3.9 all-to-all-done.7
  509.8 18.2 %reduce-scatter.4.cloned.1.call-done = bf16[384,256]{1,0:T(8,128)(2,1)} async-done(((bf16[3072,256]{1,0:T(8,128)(2,1)}), bf16[384,256]{1,0:T(8,128)(2,1)}) %reduce-scatter.4.cloned.1.call-update) | async-done | bytes 196624
  528.0 1.7 copy.160
  (126 shorter events, 17.5 us)
Async XLA Ops:
  7.2 20.2 %copy-start.13 = (bf16[1,1,256,256]{3,2,1,0:T(8,128)(2,1)S(1)}, bf16[1,1,256,256]{3,2,1,0:T(8,128)(2,1)}, u32[]{:S(2)}) copy-start(bf16[1,1,256,256]{3,2,1,0:T(8,128)(2,1)} %param.15) | copy-start | bytes 393220
  7.2 36.7 %copy-start.14 = (bf16[1,1,256,256]{3,2,1,0:T(8,128)(2,1)S(1)}, bf16[1,1,256,256]{3,2,1,0:T(8,128)(2,1)}, u32[]{:S(2)}) copy-start(bf16[1,1,256,256]{3,2,1,0:T(8,128)(2,1)} %param.16) | copy-start | bytes 393220
  7.2 85.2 %all-gather.7.cloned.1.call-start = ((), (), s32[]{:S(2)}) async-start(), calls=%async_computation.11 | async-start | bytes 1769472 | tf_op jit(solution)/shard_map/all_gather | solution.py:136
  11.7 24.2 %all-to-all-start = ((bf16[16,2,2048]{2,1,0:T(2,128)(2,1)}), bf16[16,2,2048]{2,1,0:T(2,128)(2,1)S(1)}, u32[]{:S(2)}, u32[]{:S(2)}) async-start(bf16[16,2,2048]{2,1,0:T(2,128)(2,1)} %reshape.314), calls=%async_computation | async-start | bytes 262144 | tf_op jit(solution)/shard_map/all_to_all | solution.py:111
  35.9 16.3 %all-to-all-start.1 = ((bf16[16,2,2048]{2,1,0:T(2,128)(2,1)}), bf16[16,2,2048]{2,1,0:T(2,128)(2,1)S(1)}, u32[]{:S(2)}, u32[]{:S(2)}) async-start(bf16[16,2,2048]{2,1,0:T(2,128)(2,1)} %reshape.312), calls=%async_computation.1 | async-start | bytes 262144 | tf_op jit(solution)/shard_map/all_to_all | solution.py:112
  52.2 16.6 %all-to-all-start.2 = ((bf16[16,2,2048]{2,1,0:T(2,128)(2,1)}), bf16[16,2,2048]{2,1,0:T(2,128)(2,1)S(1)}, u32[]{:S(2)}, u32[]{:S(2)}) async-start(bf16[16,2,2048]{2,1,0:T(2,128)(2,1)} %reshape.310), calls=%async_computation.2 | async-start | bytes 262144 | tf_op jit(solution)/shard_map/all_to_all | solution.py:113
  60.4 153.1 %all-gather.11.cloned.1.call-start = ((), (), s32[]{:S(2)}) async-start(), calls=%async_computation.13 | async-start | bytes 2228224 | tf_op jit(solution)/shard_map/all_gather | solution.py:157
  61.2 9.9 %copy-start.4 = (bf16[16,16,2,128]{3,2,1,0:T(2,128)(2,1)}, bf16[16,16,2,128]{3,2,1,0:T(2,128)(2,1)S(1)}, u32[]{:S(2)}) copy-start(bf16[16,16,2,128]{3,2,1,0:T(2,128)(2,1)S(1)} %reshape.282) | copy-start | bytes 393220
  69.7 17.9 %copy-start.15 = (bf16[1,1,256,256]{3,2,1,0:T(8,128)(2,1)S(1)}, bf16[1,1,256,256]{3,2,1,0:T(8,128)(2,1)}, u32[]{:S(2)}) copy-start(bf16[1,1,256,256]{3,2,1,0:T(8,128)(2,1)} %param.10) | copy-start | bytes 393220
  69.7 18.1 %copy-start.20 = (bf16[16,16,2,128]{3,2,1,0:T(2,128)(2,1)}, bf16[16,16,2,128]{3,2,1,0:T(2,128)(2,1)S(1)}, u32[]{:S(2)}) copy-start(bf16[16,16,2,128]{3,2,1,0:T(2,128)(2,1)S(1)} %reshape.284) | copy-start | bytes 393220
  69.8 17.9 %copy-start.16 = (bf16[1,1,256,256]{3,2,1,0:T(8,128)(2,1)S(1)}, bf16[1,1,256,256]{3,2,1,0:T(8,128)(2,1)}, u32[]{:S(2)}) copy-start(bf16[1,1,256,256]{3,2,1,0:T(8,128)(2,1)} %param.11) | copy-start | bytes 393220
  69.8 18.1 %copy-start.29 = (s32[1,1,2,2,2]{4,3,2,1,0:T(2,128)S(1)}, s32[1,1,2,2,2]{4,3,2,1,0:T(2,128)}, u32[]{:S(2)}) copy-start(s32[1,1,2,2,2]{4,3,2,1,0:T(2,128)} %param.13) | copy-start | bytes 100
  70.1 0.7 copy-start.11
  70.8 17.9 %copy-start.17 = (bf16[1,1,256,256]{3,2,1,0:T(8,128)(2,1)S(1)}, bf16[1,1,256,256]{3,2,1,0:T(8,128)(2,1)}, u32[]{:S(2)}) copy-start(bf16[1,1,256,256]{3,2,1,0:T(8,128)(2,1)} %param.12) | copy-start | bytes 393220
  87.5 224.3 %all-gather.9.cloned.1.call-start = ((), (), s32[]{:S(2)}) async-start(), calls=%async_computation.12 | async-start | bytes 2228224 | tf_op jit(solution)/shard_map/all_gather | solution.py:151
  87.7 2.8 copy-start.7
  87.8 2.7 copy-start.9
  88.7 1.8 copy-start.18
  88.8 1.8 copy-start.22
  90.0 2.2 copy-start.26
  90.0 1.5 copy-start.24
  90.0 1.5 copy-start.25
  91.4 336.3 %all-gather.5.cloned.1.call-start = ((), (), s32[]{:S(2)}) async-start(), calls=%async_computation.10 | async-start | bytes 3342336 | tf_op jit(solution)/shard_map/all_gather | solution.py:127
  92.1 412.1 %all-reduce.3.cloned.1.call-start = ((), (), s32[]{:S(2)}) async-start(), calls=%async_computation.15 | async-start | bytes 393216 | tf_op jit(solution)/shard_map/psum | solution.py:162
  213.4 98.5 %copy-start.2 = (bf16[1,1,256,3072]{2,3,0,1:T(8,128)(2,1)S(1)}, bf16[1,1,256,3072]{2,3,0,1:T(8,128)(2,1)}, u32[]{:S(2)}) copy-start(bf16[1,1,256,3072]{2,3,0,1:T(8,128)(2,1)} %copy.161) | copy-start | bytes 4718596
  314.7 213.3 %reduce-scatter.4.cloned.1.call-start = ((), (), s32[]{:S(2)}) async-start(), calls=%async_computation.14 | async-start | bytes 1769472
  427.6 2.4 copy-start
  427.6 2.4 copy-start.3
  432.2 17.4 %copy-start.1 = (bf16[2,256,3072]{1,2,0:T(8,128)(2,1)S(1)}, bf16[2,256,3072]{1,2,0:T(8,128)(2,1)}, u32[]{:S(2)}) copy-start(bf16[2,256,3072]{1,2,0:T(8,128)(2,1)} %all-gather.5.cloned.1.call-done) | copy-start | bytes 9437188
  440.2 17.5 %all-to-all-start.4 = ((bf16[16,2,2048]{2,1,0:T(2,128)(2,1)}), bf16[16,2,2048]{2,1,0:T(2,128)(2,1)S(1)}, u32[]{:S(2)}, u32[]{:S(2)}) async-start(bf16[16,2,2048]{2,1,0:T(2,128)(2,1)} %reshape.316), calls=%async_computation.4 | async-start | bytes 262144 | tf_op jit(solution)/shard_map/all_to_all | solution.py:171
  449.5 2.1 copy-start.6
  449.6 2.1 copy-start.23
  449.6 2.1 copy-start.27
  451.7 0.7 copy-start.30
  451.9 6.7 %copy-start.12 = (f32[16,2,16,16]{2,3,1,0:T(8,128)S(1)}, f32[16,2,16,16]{2,3,1,0:T(8,128)}, u32[]{:S(2)}) copy-start(f32[16,2,16,16]{2,3,1,0:T(8,128)} %copy-done.11) | copy-start | bytes 98308
  451.9 6.7 %copy-start.21 = (bf16[16,16,2,128]{3,2,1,0:T(2,128)(2,1)S(1)}, bf16[16,16,2,128]{3,2,1,0:T(2,128)(2,1)}, u32[]{:S(2)}) copy-start(bf16[16,16,2,128]{3,2,1,0:T(2,128)(2,1)} %copy-done.20) | copy-start | bytes 393220
  452.4 6.6 %copy-start.5 = (bf16[16,16,2,128]{3,2,1,0:T(2,128)(2,1)S(1)}, bf16[16,16,2,128]{3,2,1,0:T(2,128)(2,1)}, u32[]{:S(2)}) copy-start(bf16[16,16,2,128]{3,2,1,0:T(2,128)(2,1)} %copy-done.4) | copy-start | bytes 393220
  458.7 9.6 %copy-start.10 = (bf16[1,1,256,256]{2,3,1,0:T(8,128)(2,1)S(1)}, bf16[1,1,256,256]{2,3,1,0:T(8,128)(2,1)}, u32[]{:S(2)}) copy-start(bf16[1,1,256,256]{2,3,1,0:T(8,128)(2,1)} %copy-done.9) | copy-start | bytes 393220
  459.0 25.8 %copy-start.8 = (bf16[1,1,256,256]{2,3,1,0:T(8,128)(2,1)S(1)}, bf16[1,1,256,256]{2,3,1,0:T(8,128)(2,1)}, u32[]{:S(2)}) copy-start(bf16[1,1,256,256]{2,3,1,0:T(8,128)(2,1)} %copy-done.7) | copy-start | bytes 393220
  460.1 16.6 %all-to-all-start.6 = ((bf16[1,16,16,256]{3,2,0,1:T(8,128)(2,1)}), bf16[1,16,16,256]{3,2,0,1:T(8,128)(2,1)S(1)}, u32[]{:S(2)}, u32[]{:S(2)}) async-start(bf16[1,16,16,256]{3,2,0,1:T(8,128)(2,1)} %bitcast.40), calls=%async_computation.6 | async-start | bytes 262144 | tf_op jit(solution)/shard_map/all_to_all | solution.py:181
  468.7 32.6 %copy-start.19 = (pred[2,256,256]{1,2,0:T(32,128)(4,1)S(1)}, pred[2,256,256]{1,2,0:T(32,128)(4,1)}, u32[]{:S(2)}) copy-start(pred[2,256,256]{1,2,0:T(32,128)(4,1)} %copy-done.18) | copy-start | bytes 393220
  468.7 32.6 %copy-start.28 = (f32[2,256]{1,0:T(2,128)S(1)}, f32[2,256]{1,0:T(2,128)}, u32[]{:S(2)}) copy-start(f32[2,256]{1,0:T(2,128)} %copy-done.26) | copy-start | bytes 6148
  468.7 32.6 %copy-start.31 = (bf16[256,256]{1,0:T(8,128)(2,1)S(1)}, bf16[256,256]{1,0:T(8,128)(2,1)}, u32[]{:S(2)}) copy-start(bf16[256,256]{1,0:T(8,128)(2,1)} %copy-done.30) | copy-start | bytes 393220
  476.7 16.6 %all-to-all-start.5 = ((bf16[1,16,16,256]{3,2,0,1:T(8,128)(2,1)}), bf16[1,16,16,256]{3,2,0,1:T(8,128)(2,1)S(1)}, u32[]{:S(2)}, u32[]{:S(2)}) async-start(bf16[1,16,16,256]{3,2,0,1:T(8,128)(2,1)} %bitcast.35), calls=%async_computation.5 | async-start | bytes 262144 | tf_op jit(solution)/shard_map/all_to_all | solution.py:178
  493.3 16.5 %all-to-all-start.7 = ((bf16[1,16,16,256]{3,2,0,1:T(8,128)(2,1)}), bf16[1,16,16,256]{3,2,0,1:T(8,128)(2,1)S(1)}, u32[]{:S(2)}, u32[]{:S(2)}) async-start(bf16[1,16,16,256]{3,2,0,1:T(8,128)(2,1)} %bitcast.44), calls=%async_computation.7 | async-start | bytes 262144 | tf_op jit(solution)/shard_map/all_to_all | solution.py:184
Sparse Core Ops, SparseCore 0:
  10.2 33.8 all-gather.6
  87.7 125.7 all-gather.10
  217.2 94.6 all-gather.8
  315.5 112.0 all-gather.4
  431.0 57.3 all-reduce.2
  491.3 36.6 reduce-scatter.3
where the time goes:
time: 541 us; the launch traced here: 539 us
  waiting for transfers between devices  309 us (57%)
  starting transfers between devices  65.8 us (12%)
  blocking collectives  59.7 us (11%)
  local copies, waits for them, and re-layouts  44.9 us (8%)
  other arithmetic  25.5 us (5%)
  matrix products  18.8 us (3%)
  between operations  14.8 us (3%)
    all_gather x1, waiting for transfers between devices, per_device(): piece = lax.all_gather(stacked, 'seq', axis=2, tiled=True)  113 us
    all_gather x1, waiting for transfers between devices, per_device(): lax.all_gather(spatial_att4, 'seq', axis=1, tiled=True)  95.1 us
    all_to_all x1, blocking collectives, per_device(): lax.all_to_all(cot_full, 'seq', split_axis=3, concat_axis=1, tiled=True)  43.4 us
    all_gather x1, waiting for transfers between devices, per_device(): lax.all_gather(t_attended, 'seq', axis=1, tiled=True)  39.9 us
    unnamed x87, local copies, waits for them, and re-layouts  28.5 us
    unnamed x5, other arithmetic  22.9 us
    unnamed x7, waiting for transfers between devices  19 us
    all_to_all x1, blocking collectives, per_device(): lax.all_to_all(t_attended_tok.reshape(token_layout), 'seq', split_axis=1,...  16.2 us
  transfers between devices with their start and end apart: 13, of which 11 were waited for; matrix products, arithmetic and copies ran while one was open for 16% of the time, Pallas kernels for 0%

commit v1 on v0

v1 whole, which is shorter than its diff:
```python
import functools
import math

import jax
import jax.numpy as jnp
from jax import lax
from jax.experimental import pallas as pl
from jax.experimental.pallas import tpu as pltpu
from jax.sharding import PartitionSpec as P

MESH = pl.DeviceIdType.MESH
BF16 = jnp.bfloat16
F32 = jnp.float32
NEG = -1e30


def dot(a, b):
    return lax.dot_general(a, b, (((1,), (0,)), ((), ())), preferred_element_type=F32)


def dot_nt(a, b):
    return lax.dot_general(a, b, (((1,), (1,)), ((), ())), preferred_element_type=F32)


def dot_tn(a, b):
    return lax.dot_general(a, b, (((0,), (0,)), ((), ())), preferred_element_type=F32)


def wait_for(view, sem):
    pltpu.make_async_copy(view, view, sem).wait()


def kernel(
    dims,
    sq, sk, sv, mask, tq, tk, tv, sp, tp, cot,
    upd, gsq, gsk, gsv, gtq, gtk, gtv, gsp, gtp,
    wts, wtt, wtmp, cotb, tqb, tkb, tvb,
    s_shares, t_shares, s_att, t_att, t_att_tok, gs_acc, gt_acc, g_t, g_tok, q_g, k_g, v_g,
    ps, pt, rs_s, rs_t, rs_s_half, rs_t_half, sec_s, sec_t, fin,
    u_out, u_in, u_keep, u_send, u_recv,
    sems,
):
    NDP, NSEQ, NHEAD, HL, HDIM, Q = dims
    Z, Y, X = NSEQ // 2, NDP * 2, NHEAD // 2
    TOK, LW = sq.shape
    TB = TOK // NSEQ
    DH = cot.shape[1]
    scale = 1.0 / math.sqrt(HDIM)

    dp = lax.axis_index("dp")
    seq = lax.axis_index("seq")
    head = lax.axis_index("head")
    z, yh = seq // 2, lax.rem(seq, 2)
    y = yh * NDP + dp
    x, core = head // 2, lax.rem(head, 2)

    def at_y(place):
        return {"dp": lax.rem(place, NDP), "seq": z * 2 + place // NDP}

    def at_z(place):
        return {"seq": place * 2 + yh}

    def at_x(place):
        return {"head": place * 2 + core}

    sibling = {"head": x * 2 + 1 - core}
    counter = iter(range(1000))

    def sem():
        return sems.at[next(counter)]

    def send(src, dst, send_sem, recv_sem, to):
        pltpu.make_async_remote_copy(
            src_ref=src, dst_ref=dst, send_sem=send_sem, recv_sem=recv_sem,
            device_id=to, device_id_type=MESH,
        ).start()

    barrier = pltpu.get_barrier_semaphore()

    def greet(to):
        pl.semaphore_signal(barrier, inc=1, device_id=to, device_id_type=MESH)

    @pl.loop(1, NSEQ)
    def _(i):
        greet({"seq": lax.rem(seq + i, NSEQ)})

    @pl.loop(1, NDP)
    def _(i):
        other = lax.rem(dp + i, NDP)
        greet({"dp": other, "seq": z * 2})
        greet({"dp": other, "seq": z * 2 + 1})

    @pl.loop(1, X)
    def _(i):
        greet(at_x(lax.rem(x + i, X)))

    greet(sibling)

    DS = sp.shape[1]
    eye = (
        lax.broadcasted_iota(jnp.int32, (DS, DS), 0) == lax.broadcasted_iota(jnp.int32, (DS, DS), 1)
    ).astype(F32).astype(BF16)
    wts[z, pl.ds(yh * NDP, NDP)] = dot_nt(eye, sp[...]).astype(BF16).reshape(NDP, Q, LW)
    wtmp[...] = dot_nt(eye, tp[...]).astype(BF16).reshape(NDP, Q, LW)
    wtt[y, z] = wtmp[dp]

    pl.semaphore_wait(barrier, NSEQ - 1 + 2 * (NDP - 1) + X)

    def all_to_all(src, dst, send_sem, recv_sem):
        mine = pl.ds(pl.multiple_of(seq * TB, TB), TB)

        @pl.loop(1, NSEQ)
        def _(i):
            other = lax.rem(seq + i, NSEQ)
            send(
                src.at[pl.ds(pl.multiple_of(other * TB, TB), TB)], dst.at[mine],
                send_sem, recv_sem, {"seq": other},
            )

    def rest(ref):
        return ref.at[pl.ds(0, (NSEQ - 1) * TB)]

    mine = pl.ds(pl.multiple_of(seq * TB, TB), TB)
    qkv = ((tq, tqb), (tk, tkb), (tv, tvb))
    qkv_s, qkv_r, qkv_l = [sem() for _ in qkv], [sem() for _ in qkv], [sem() for _ in qkv]
    for (src, dst), s, r, l in zip(qkv, qkv_s, qkv_r, qkv_l):
        all_to_all(src, dst, s, r)
        pltpu.make_async_copy(src.at[mine], dst.at[mine], l).start()

    mir_s, mir_r = sem(), sem()
    own_s = wts.at[z, pl.ds(yh * NDP, NDP)]
    send(own_s, own_s, mir_s, mir_r, {"dp": NDP - 1 - dp, "seq": z * 2 + 1 - yh})

    zq_s, zq_r = sem(), sem()

    @pl.loop(1, Z)
    def _(i):
        send(wtt.at[y, z], wtt.at[y, z], zq_s, zq_r, at_z(lax.rem(z + i, Z)))

    cot_l, cot_s = sem(), [sem() for _ in range(X)]
    cot_r = [sem() for _ in range(X - 1)]
    cot_sib = sem()
    pltpu.make_async_copy(cot, cotb.at[head], cot_l).start()
    for i in range(1, X):
        send(cot, cotb.at[head], cot_s[i - 1], cot_r[i - 1], at_x(lax.rem(x + i, X)))
    send(cot, cotb.at[head], cot_s[X - 1], cot_sib, sibling)

    def heads(ref, h):
        return ref[:, h * HDIM : (h + 1) * HDIM]

    def forward(h, q, k, v, bias, shares):
        scores = dot_nt(heads(q, h), heads(k, h)) * scale + bias
        e = jnp.exp(scores - jnp.max(scores, axis=-1, keepdims=True))
        part = e * (1.0 / jnp.sum(e, axis=-1, keepdims=True))
        shares[h] = part
        return dot(part.astype(BF16), heads(v, h)).astype(BF16)

    def backward(h, q, k, v, g, shares):
        share = shares[h]
        weight = share.astype(BF16)
        grad = heads(g, h)
        grad_shares = dot_nt(grad, heads(v, h))
        centre = jnp.sum(share * grad_shares, axis=-1, keepdims=True)
        grad_scores = (share * (grad_shares - centre)).astype(BF16)
        dq = (dot(grad_scores, heads(k, h)) * scale).astype(BF16)
        dk = (dot_tn(grad_scores, heads(q, h)) * scale).astype(BF16)
        dv = dot_tn(weight, grad).astype(BF16)
        return dq, dk, dv

    NB = mask.shape[-1]
    tile = TOK // NB
    rows = lax.broadcasted_iota(jnp.int32, (TOK, TOK), 0)
    cols = lax.broadcasted_iota(jnp.int32, (TOK, TOK), 1)
    for h in range(HL):
        bias = jnp.zeros((TOK, TOK), F32)
        for a in range(NB):
            for b in range(NB):
                value = (mask[0, 0, h, a, b].astype(F32) - 1.0) * -NEG
                inside = jnp.logical_and(rows // tile == a, cols // tile == b)
                bias = jnp.where(inside, value, bias)
        s_att[:, h * HDIM : (h + 1) * HDIM] = forward(h, sq, sk, sv, bias, s_shares)

    def ring_ids(n, me, where):
        return where(lax.rem(me + 1, n)), where(lax.rem(me + n - 1, n))

    class Gather:
        def __init__(self, buf, n, me, where):
            self.buf, self.n, self.me = buf, n, me
            self.right, self.left = ring_ids(n, me, where)
            self.half = n // 2
            self.s = [[sem() for _ in range(self.half)] for _ in range(2)]
            self.r = [[sem() for _ in range(self.half)] for _ in range(2)]

        def view(self, way, step, k):
            sign = -1 if way == 0 else 1
            chunk = lax.rem(self.me + sign * k + self.n, self.n)
            if step < self.half:
                return self.buf.at[chunk]
            size = self.buf.shape[1] // 2
            return self.buf.at[chunk, pl.ds(way * size, size)]

        def start(self, step):
            for way, to in ((0, self.right), (1, self.left)):
                if step > 1:
                    wait_for(self.view(way, step - 1, step - 1), self.r[way][step - 2])
                v = self.view(way, step, step - 1)
                send(v, v, self.s[way][step - 1], self.r[way][step - 1], to)

        def finish(self):
            for way in range(2):
                wait_for(self.view(way, self.half, self.half), self.r[way][self.half - 1])

        def drain(self):
            for way in range(2):
                for step in range(1, self.half + 1):
                    wait_for(self.view(way, step, step - 1), self.s[way][step - 1])

    class Scatter:
        def __init__(self, buf, arrive, arrive_half, n, me, where):
            self.buf, self.n, self.me = buf, n, me
            self.arrive, self.arrive_half = arrive, arrive_half
            self.right, self.left = ring_ids(n, me, where)
            self.half = n // 2
            self.s = [[sem() for _ in range(self.half)] for _ in range(2)]
            self.r = [[sem() for _ in range(self.half)] for _ in range(2)]

        def dest(self, way, step):
            sign = 1 if way == 0 else -1
            return lax.rem(self.me + sign * (self.half + 1 - step) + self.n, self.n)

        def source(self, way, step):
            if step > 1:
                return self.buf.at[self.dest(way, step)]
            size = self.buf.shape[1] // 2
            return self.buf.at[self.dest(way, 1), pl.ds(way * size, size)]

        def landing(self, way, step):
            return self.arrive_half.at[way] if step == 1 else self.arrive.at[way, step - 2]

        def start(self, step):
            for way, to in ((0, self.right), (1, self.left)):
                if step > 1:
                    landed = self.landing(way, step - 1)
                    wait_for(landed, self.r[way][step - 2])
                    d = self.dest(way, step)
                    size = self.buf.shape[1] // 2
                    where = pl.ds(way * size, size) if step == 2 else pl.ds(0, 2 * size)
                    total = self.buf[d, where].astype(F32) + landed[...].astype(F32)
                    self.buf[d, where] = total.astype(BF16)
                send(
                    self.source(way, step), self.landing(way, step),
                    self.s[way][step - 1], self.r[way][step - 1], to,
                )

        def finish(self):
            total = self.buf[self.me].astype(F32)
            for way in range(2):
                landed = self.landing(way, self.half)
                wait_for(landed, self.r[way][self.half - 1])
                total = total + landed[...].astype(F32)
            self.buf[self.me] = total.astype(BF16)

        def drain(self):
            for way in range(2):
                for step in range(1, self.half + 1):
                    wait_for(self.source(way, step), self.s[way][step - 1])

    wz = Gather(wts, Z, z, at_z)
    wy = Gather(wtt, Y, y, at_y)
    wait_for(own_s, mir_r)
    wz.start(1)
    wait_for(wtt.at[y, pl.ds(0, Z - 1)], zq_r)
    wy.start(1)

    for (src, dst), r, l in zip(qkv, qkv_r, qkv_l):
        wait_for(rest(dst), r)
        wait_for(dst.at[mine], l)
    same = jnp.where(lax.rem(rows, TB) == lax.rem(cols, TB), 0.0, NEG).astype(F32)
    for h in range(HL):
        t_att_tok[:, h * HDIM : (h + 1) * HDIM] = forward(h, tqb, tkb, tvb, same, t_shares)
    ta_s, ta_r = sem(), sem()
    all_to_all(t_att_tok, t_att, ta_s, ta_r)
    t_att[mine] = t_att_tok[mine]

    fwd_s, fwd_r = [sem() for _ in range(X - 1)], [sem() for _ in range(X - 1)]
    for i in range(1, X):
        slot = cotb.at[lax.rem(x + X - i, X) * 2 + core]
        wait_for(slot, cot_r[i - 1])
        send(slot, slot, fwd_s[i - 1], fwd_r[i - 1], sibling)

    wz.start(2)
    wy.start(2)
    wait_for(cotb.at[head], cot_l)
    wait_for(cotb.at[head], cot_sib)
    for i in range(1, X):
        wait_for(cotb.at[head], fwd_r[i - 1])

    @pl.loop(0, Z)
    def _(b):
        ps[b] = dot_tn(cotb[b], s_att[...]).astype(BF16).reshape(Y, Q, LW)

    wz.start(3) if wz.half >= 3 else None
    wy.start(3) if wy.half >= 3 else None
    wait_for(rest(t_att), ta_r)

    @pl.loop(0, Z)
    def _(b):
        pt[:, pl.ds(b, 1)] = dot_tn(cotb[b], t_att[...]).astype(BF16).reshape(Y, 1, Q, LW)

    for step in range(4, wz.half + 1):
        wz.start(step)
        wy.start(step)
    wz.finish()
    wy.finish()

    gs_acc[...] = jnp.zeros_like(gs_acc)
    gt_acc[...] = jnp.zeros_like(gt_acc)

    def block_t(b):
        return wtt[:, pl.ds(b, 1)].reshape(DH, LW)

    def block_s(b):
        return wts[b].reshape(DH, LW)

    @pl.loop(0, Z)
    def _(b):
        gt_acc[...] += dot(cotb[b], block_t(b))
        gs_acc[...] += dot(cotb[b], block_s(b))

    g_t[...] = gt_acc[...].astype(BF16)
    gt_s, gt_r = sem(), sem()
    all_to_all(g_t, g_tok, gt_s, gt_r)
    g_tok[mine] = g_t[mine]

    rz = Scatter(ps, rs_s, rs_s_half, Z, z, at_z)
    ry = Scatter(pt, rs_t, rs_t_half, Y, y, at_y)
    rz.start(1)
    ry.start(1)

    def update(b):
        return dot_nt(s_att[...], block_s(b)) + dot_nt(t_att[...], block_t(b))

    us_s, us_r = sem(), sem()

    @pl.loop(0, X)
    def _(i):
        u_out[i] = update(i * 2 + 1 - core).astype(BF16)
        send(u_out.at[i], u_in.at[i], us_s, us_r, sibling)

    rz.start(2)
    ry.start(2)

    @pl.loop(0, X)
    def _(i):
        u_keep[i] = update(i * 2 + core)

    wait_for(u_in, us_r)
    ux_s, ux_r = sem(), sem()

    @pl.loop(1, X)
    def _(i):
        other = lax.rem(x + i, X)
        u_send[i - 1] = (u_keep[other] + u_in[other].astype(F32)).astype(BF16)
        send(u_send.at[i - 1], u_recv.at[i - 1], ux_s, ux_r, at_x(other))

    g_s = gs_acc[...].astype(BF16)
    for h in range(HL):
        f = slice(h * HDIM, (h + 1) * HDIM)
        gsq[:, f], gsk[:, f], gsv[:, f] = backward(h, sq, sk, sv, g_s, s_shares)

    rz.start(3) if rz.half >= 3 else None
    ry.start(3) if ry.half >= 3 else None

    wait_for(rest(g_tok), gt_r)
    for h in range(HL):
        f = slice(h * HDIM, (h + 1) * HDIM)
        q_g[:, f], k_g[:, f], v_g[:, f] = backward(h, tqb, tkb, tvb, g_tok, t_shares)
    grads = ((q_g, gtq), (k_g, gtk), (v_g, gtv))
    grads_s, grads_r = [sem() for _ in grads], [sem() for _ in grads]
    for (src, dst), s, r in zip(grads, grads_s, grads_r):
        all_to_all(src, dst, s, r)
        dst[mine] = src[mine]

    for step in range(4, rz.half + 1):
        rz.start(step)
        ry.start(step)

    wait_for(u_recv, ux_r)
    total = u_keep[x] + u_in[x].astype(F32)
    for i in range(X - 1):
        total = total + u_recv[i].astype(F32)
    upd[...] = total.astype(BF16)

    rz.finish()
    sec_ss, sec_sr = sem(), sem()

    @pl.loop(1, Y)
    def _(i):
        other = lax.rem(y + i, Y)
        send(ps.at[z, other], sec_s.at[i - 1], sec_ss, sec_sr, at_y(other))

    ry.finish()
    sec_ts, sec_tr = sem(), sem()

    @pl.loop(1, Z)
    def _(i):
        other = lax.rem(z + i, Z)
        send(pt.at[y, other], sec_t.at[i - 1], sec_ts, sec_tr, at_z(other))

    wait_for(sec_s, sec_sr)
    total = ps[z, y].astype(F32)
    for i in range(Y - 1):
        total = total + sec_s[i].astype(F32)
    fin[dp, 0] = total * (1.0 / NDP)
    wait_for(sec_t, sec_tr)
    total = pt[y, z].astype(F32)
    for i in range(Z - 1):
        total = total + sec_t[i].astype(F32)
    fin[dp, 1] = total * (1.0 / NDP)

    fin_s, fin_r = sem(), sem()

    @pl.loop(1, NDP)
    def _(i):
        send(fin.at[dp], fin.at[dp], fin_s, fin_r, {"dp": lax.rem(dp + i, NDP)})

    for (src, dst), r in zip(grads, grads_r):
        wait_for(rest(dst), r)

    for (src, dst), s in zip(qkv, qkv_s):
        wait_for(rest(dst), s)
    wait_for(own_s, mir_s)
    wait_for(wtt.at[y, pl.ds(0, Z - 1)], zq_s)
    for s in cot_s + fwd_s:
        wait_for(cotb.at[head], s)
    wz.drain()
    wy.drain()
    rz.drain()
    ry.drain()
    for s in (ta_s, gt_s):
        wait_for(rest(t_att), s)
    for s in grads_s:
        wait_for(rest(t_att), s)
    wait_for(u_in, us_s)
    wait_for(u_recv, ux_s)
    wait_for(sec_s, sec_ss)
    wait_for(sec_t, sec_ts)
    wait_for(fin.at[pl.ds(0, NDP - 1)], fin_r)
    wait_for(fin.at[pl.ds(0, NDP - 1)], fin_s)
    gsp[...] = fin[:, 0].reshape(DS, LW)
    gtp[...] = fin[:, 1].reshape(DS, LW)


def per_device(dims, *args):
    NDP, NSEQ, NHEAD = dims
    sq, sk, sv, mask, tq, tk, tv, sp, tp, cot = args
    tokens, width = sq.shape[2:]
    HL = mask.shape[2]
    HDIM = width // HL
    DS, DH = sp.shape[1], cot.shape[3]
    Z, Y, X = NSEQ // 2, NDP * 2, NHEAD // 2
    Q = DS // NDP
    flat = [a.reshape(a.shape[2:]) for a in (sq, sk, sv, tq, tk, tv, cot)]
    vmem = pl.BlockSpec(memory_space=pltpu.VMEM)
    hbm = pl.BlockSpec(memory_space=pl.ANY)
    feat = jax.ShapeDtypeStruct((tokens, width), BF16)
    proj = jax.ShapeDtypeStruct((DS, width), F32)

    def buf(*shape, dtype=BF16):
        return pltpu.VMEM(shape, dtype)

    feats = functools.partial(buf, tokens, width)
    out = pl.pallas_call(
        functools.partial(kernel, (NDP, NSEQ, NHEAD, HL, HDIM, Q)),
        out_shape=[jax.ShapeDtypeStruct((tokens, DH), BF16)] + [feat] * 6 + [proj] * 2,
        in_specs=[vmem] * 3 + [pl.BlockSpec(memory_space=pltpu.SMEM)] + [hbm] * 3 + [vmem] * 2 + [hbm],
        out_specs=[vmem] * 9,
        scratch_shapes=[
            buf(Z, Y, Q, width),
            buf(Y, Z, Q, width),
            buf(NDP, Q, width),
            buf(NHEAD, tokens, DH),
            feats(), feats(), feats(),
            buf(HL, tokens, tokens, dtype=F32),
            buf(HL, tokens, tokens, dtype=F32),
            feats(), feats(), feats(),
            feats(dtype=F32), feats(dtype=F32),
            feats(), feats(), feats(), feats(), feats(),
            buf(Z, Y, Q, width),
            buf(Y, Z, Q, width),
            buf(2, Z // 2 - 1, Y, Q, width),
            buf(2, Y // 2 - 1, Z, Q, width),
            buf(2, Y // 2, Q, width),
            buf(2, Z // 2, Q, width),
            buf(Y - 1, Q, width),
            buf(Z - 1, Q, width),
            buf(NDP, 2, Q, width, dtype=F32),
            buf(X, tokens, DH),
            buf(X, tokens, DH),
            buf(X, tokens, DH, dtype=F32),
            buf(X - 1, tokens, DH),
            buf(X - 1, tokens, DH),
            pltpu.SemaphoreType.DMA((128,)),
        ],
        compiler_params=pltpu.CompilerParams(
            collective_id=0, has_side_effects=True, vmem_limit_bytes=48 * 1024 * 1024
        ),
    )(flat[0], flat[1], flat[2], mask, flat[3], flat[4], flat[5], sp, tp, flat[6])
    return tuple(o[None, None] for o in out[:7]) + (out[7].T, out[8].T)


def solution(mesh):
    tokens = P("dp", "seq", None, "head")
    weights = P("head", "seq")
    dims = tuple(mesh.shape[a] for a in ("dp", "seq", "head"))
    return jax.shard_map(
        functools.partial(per_device, dims),
        mesh=mesh,
        in_specs=(tokens,) * 3 + (P("dp", "seq", "head", None, None),) + (tokens,) * 3 + (weights,) * 2 + (tokens,),
        out_specs=(tokens,) * 7 + (weights,) * 2,
        check_vma=False,
    )
```

time: 541 us -> 119 us (0.22)
  waiting for transfers between devices: 309 us -> 0 us
  Pallas kernels: 0 us -> 106 us
  starting transfers between devices: 65.8 us -> 0 us
  blocking collectives: 59.7 us -> 0 us
  local copies, waits for them, and re-layouts: 44.9 us -> 11.7 us
  other arithmetic: 25.5 us -> 0 us
  matrix products: 18.8 us -> 0 us
  between operations: 14.8 us -> 0.74 us
    all_gather x4 -> x0, waiting for transfers between devices: 248 us -> none  [the longest x1 113 us: per_device(): piece = lax.all_gather(stacked, 'seq', axis=2, tiled=True)]
    pallas_call x0 -> x1, Pallas kernels: none -> 106 us  [per_device(): pl.pallas_call(functools.partial(kernel, (NDP, NSEQ, NHEAD, HL, HDIM, Q))...]
    all_to_all x7 -> x0, starting transfers between devices: 65.4 us -> none  [the longest x1 15.7 us: per_device(): lax.all_to_all(temporal_query, 'seq', split_axis=2, concat_axis=1, tiled=...]
    all_to_all x2 -> x0, blocking collectives: 59.7 us -> none  [the longest x1 43.4 us: per_device(): lax.all_to_all(cot_full, 'seq', split_axis=3, concat_axis=1, tiled=True)]
    all_to_all x7 -> x0, waiting for transfers between devices: 42.3 us -> none  [the longest x1 7.17 us: per_device(): lax.all_to_all(tq_grad.reshape(token_layout), 'seq', split_axis=1, concat...]
    unnamed x5 -> x0, other arithmetic: 22.9 us -> none
    unnamed x7 -> x0, waiting for transfers between devices: 19 us -> none
    dot_general x16 -> x0, matrix products: 17.3 us -> none  [the longest x1 3.4 us: per_device(): jnp.einsum('cftk,cftd->kd', lax.all_gather(t_attended, 'seq', axis=1, til...]
  transfers between devices with their start and end apart: 13 -> 0, of which waited for: 11 -> 0; matrix products, arithmetic and copies ran while one was open for 16% -> 0% of each run, Pallas kernels for 0% -> 0%
where the time goes in v1:
time: 119 us
  Pallas kernels  106 us (89%)
  local copies, waits for them, and re-layouts  11.7 us (10%)
    pallas_call x1, Pallas kernels, per_device(): pl.pallas_call(functools.partial(kernel, (NDP, NSEQ, NHEAD, HL, HDIM, Q))...  106 us
    unnamed x27, local copies, waits for them, and re-layouts  11.7 us

profile of v1, /device:TPU:56, one launch (start us, length us, event | category | flops | bytes accessed | tf_op | source)
XLA Modules:
  0.0 118.6 jit_solution(11483361890823934411)
XLA Ops:
  0.6 0.0 copy-start.7
  0.7 0.0 copy-start
  0.7 0.0 copy-start.2
  0.7 1.0 copy.19.sp
  1.7 0.0 copy-start.1
  1.7 1.0 copy.20.tp
  2.8 0.0 copy-done.7
  2.8 0.0 copy-done
  2.8 0.0 copy-done.2
  2.8 0.0 copy-done.1
  2.8 0.0 copy-start.3
  2.8 0.9 copy-done.3
  3.7 0.0 copy-start.4
  3.7 0.9 copy-done.4
  4.6 0.0 copy-start.5
  4.6 0.9 copy-done.5
  5.5 0.0 copy-start.6
  5.5 0.9 copy-done.6
  6.4 106.2 %shard_map.169 = (bf16[256,384]{1,0:T(8,128)(2,1)S(1)}, bf16[256,256]{1,0:T(8,128)(2,1)S(1)}, bf16[256,256]{1,0:T(8,128)(2,1)S(1)}, bf16[256,256]{1,0:T(8,128)(2...) custom-call(bf16[256,256]{1,0:T(8,128)(2,1)S(1)} %bitcast.20, ...), custom_call_target="tpu_custom_call" | custom-call | tf_op jit(solution)/shard_map/pallas_call | solution.py:473
  112.7 0.7 copy.30
  113.4 0.7 copy.31
  114.0 0.7 copy.32
  114.7 0.7 copy.33
  115.3 0.7 copy.34
  116.0 0.7 copy.35
  116.6 0.7 copy.36
  117.3 0.7 copy.37
  118.0 0.7 copy.38
Async XLA Ops:
  0.6 2.1 %copy-start.7 = (s32[1,1,2,2,2]{4,3,2,1,0:T(2,128)S(1)}, s32[1,1,2,2,2]{4,3,2,1,0:T(2,128)}, u32[]{:S(2)}) copy-start(s32[1,1,2,2,2]{4,3,2,1,0:T(2,128)} %mask.1) | copy-start | bytes 100
  0.7 2.1 %copy-start = (bf16[1,1,256,384]{3,2,1,0:T(8,128)(2,1)S(1)}, bf16[1,1,256,384]{3,2,1,0:T(8,128)(2,1)}, u32[]{:S(2)}) copy-start(bf16[1,1,256,384]{3,2,1,0:T(8,128)(2,1)} %param.19) | copy-start | bytes 589828
  0.7 2.1 %copy-start.2 = (bf16[1,1,256,256]{3,2,1,0:T(8,128)(2,1)S(1)}, bf16[1,1,256,256]{3,2,1,0:T(8,128)(2,1)}, u32[]{:S(2)}) copy-start(bf16[1,1,256,256]{3,2,1,0:T(8,128)(2,1)} %param.11) | copy-start | bytes 393220
  1.7 1.1 copy-start.1
  2.8 0.9 copy-start.3
  3.7 0.9 copy-start.4
  4.6 0.9 copy-start.5
  5.5 0.9 copy-start.6

commit v2 on v1

v2 whole, which is shorter than its diff:
```python
import functools
import math

import jax
import jax.numpy as jnp
from jax import lax
from jax.experimental import pallas as pl
from jax.experimental.pallas import tpu as pltpu
from jax.sharding import PartitionSpec as P

MESH = pl.DeviceIdType.MESH
BF16 = jnp.bfloat16
F32 = jnp.float32
NEG = -1e30
SEMS = 192


def dot(a, b):
    return lax.dot_general(a, b, (((1,), (0,)), ((), ())), preferred_element_type=F32)


def dot_nt(a, b):
    return lax.dot_general(a, b, (((1,), (1,)), ((), ())), preferred_element_type=F32)


def dot_tn(a, b):
    return lax.dot_general(a, b, (((0,), (0,)), ((), ())), preferred_element_type=F32)


def wait_for(view, sem):
    pltpu.make_async_copy(view, view, sem).wait()


def kernel(
    dims,
    sq_in, sk_in, sv_in, mask, tq, tk, tv, sp, tp, cot,
    upd, gsq, gsk, gsv, gtq, gtk, gtv, gsp, gtp,
    sq, sk, sv, wts, wtt, cotb, tqb, tkb, tvb,
    s_shares, t_shares, s_att, t_att, t_att_tok, gs_acc, gt_acc, g_t, g_tok, q_g, k_g, v_g,
    ps, pt, rs_s, rs_t, sec_s, sec_t, fin,
    u_out, u_in, u_keep, u_send, u_recv,
    sems,
):
    NDP, NSEQ, NHEAD, HL, HDIM, Q = dims
    Z, Y, X = NSEQ // 2, NDP * 2, NHEAD // 2
    TOK, LW = sq.shape
    DS = NDP * Q
    TB = TOK // NSEQ
    DH = cot.shape[1]
    scale = 1.0 / math.sqrt(HDIM)

    dp = lax.axis_index("dp")
    seq = lax.axis_index("seq")
    head = lax.axis_index("head")
    z, yh = seq // 2, lax.rem(seq, 2)
    y = yh * NDP + dp
    x, core = head // 2, lax.rem(head, 2)

    def at_y(place):
        return {"dp": lax.rem(place, NDP), "seq": z * 2 + place // NDP}

    def at_z(place):
        return {"seq": place * 2 + yh}

    def at_x(place):
        return {"head": place * 2 + core}

    sibling = {"head": x * 2 + 1 - core}
    counter = iter(range(SEMS))

    def sem(part):
        return sems.at[next(counter)]

    def local(src, dst, done):
        pltpu.make_async_copy(src, dst, done).start()

    def send(src, dst, send_sem, recv_sem, to):
        pltpu.make_async_remote_copy(
            src_ref=src, dst_ref=dst, send_sem=send_sem, recv_sem=recv_sem,
            device_id=to, device_id_type=MESH,
        ).start()

    barrier = pltpu.get_barrier_semaphore()

    def greet(to):
        pl.semaphore_signal(barrier, inc=1, device_id=to, device_id_type=MESH)

    @pl.loop(1, NSEQ)
    def _(i):
        greet({"seq": lax.rem(seq + i, NSEQ)})

    @pl.loop(1, NDP)
    def _(i):
        other = lax.rem(dp + i, NDP)
        greet({"dp": other, "seq": z * 2})
        greet({"dp": other, "seq": z * 2 + 1})

    @pl.loop(1, X)
    def _(i):
        greet(at_x(lax.rem(x + i, X)))

    greet(sibling)

    spatial = ((sq_in, sq), (sk_in, sk), (sv_in, sv))
    spatial_l = [sem("in") for _ in spatial]
    for (src, dst), l in zip(spatial, spatial_l):
        local(src, dst, l)
    own_l, cot_l = [sem("in") for _ in range(2)], sem("in")
    own_s = wts.at[z, pl.ds(yh * NDP, NDP)]
    local(sp, own_s, own_l[0])
    local(tp.at[dp], wtt.at[y, 1], own_l[1])
    local(cot, cotb.at[head], cot_l)

    pl.semaphore_wait(barrier, NSEQ - 1 + 2 * (NDP - 1) + X)

    def spatial_piece(chunk, piece):
        return wts.at[chunk, pl.ds((yh if piece == 0 else 1 - yh) * NDP, NDP)]

    def temporal_piece(chunk, piece):
        return wtt.at[chunk, pl.ds(piece * (Z // 2), Z // 2)]

    zq_s, zq_r = sem("w"), [sem("w"), sem("w")]
    for i in range(1, Z):
        slot = (1 - i) % Z
        send(tp.at[dp], wtt.at[y, slot], zq_s, zq_r[slot // (Z // 2)], at_z(lax.rem(z + i, Z)))

    mir_s, mir_r = sem("w"), sem("w")
    send(sp, own_s, mir_s, mir_r, {"dp": NDP - 1 - dp, "seq": z * 2 + 1 - yh})

    class Ring:
        def __init__(self, part, n, me, where):
            self.n, self.me = n, me
            self.to = where(lax.rem(me + 1, n)), where(lax.rem(me + n - 1, n))
            self.sems = {
                (way, piece): [(sem(part), sem(part)) for _ in range(self.hops(way, piece))]
                for way in range(2) for piece in range(2)
            }

        def hops(self, way, piece):
            return self.n // 2 if way == piece else self.n // 2 - 1

        def place(self, way, k):
            return lax.rem(self.me + (k if way == 0 else -k) + self.n, self.n)

    class Gather(Ring):
        def __init__(self, part, n, me, where, view):
            super().__init__(part, n, me, where)
            self.view = view

        def arrived(self, way, piece, j):
            wait_for(self.view(self.place(way, -j), piece), self.sems[way, piece][j - 1][1])

        def hop(self, piece, j):
            for way in range(2):
                if j <= self.hops(way, piece):
                    if j > 1:
                        self.arrived(way, piece, j - 1)
                    v = self.view(self.place(way, 1 - j), piece)
                    send(v, v, *self.sems[way, piece][j - 1], self.to[way])

        def finish(self):
            for piece in range(2):
                for way in range(2):
                    self.arrived(way, piece, self.hops(way, piece))

        def drain(self):
            for (way, piece), pairs in self.sems.items():
                for s, _ in pairs:
                    wait_for(self.view(self.me, piece), s)

    wz = Gather("w", Z, z, at_z, spatial_piece)
    wy = Gather("w", Y, y, at_y, temporal_piece)
    wait_for(own_s, own_l[0])
    wz.hop(0, 1)

    def all_to_all(src, dst, send_sem, recv_sem):
        mine = pl.ds(pl.multiple_of(seq * TB, TB), TB)

        @pl.loop(1, NSEQ)
        def _(i):
            other = lax.rem(seq + i, NSEQ)
            send(
                src.at[pl.ds(pl.multiple_of(other * TB, TB), TB)], dst.at[mine],
                send_sem, recv_sem, {"seq": other},
            )

    def rest(ref):
        return ref.at[pl.ds(0, (NSEQ - 1) * TB)]

    mine = pl.ds(pl.multiple_of(seq * TB, TB), TB)
    qkv = ((tq, tqb), (tk, tkb), (tv, tvb))
    qkv_s, qkv_r, qkv_l = [[sem("qkv") for _ in qkv] for _ in range(3)]
    for (src, dst), s, r, l in zip(qkv, qkv_s, qkv_r, qkv_l):
        all_to_all(src, dst, s, r)
        local(src.at[mine], dst.at[mine], l)

    cot_s = [sem("cot") for _ in range(X)]
    cot_r = [sem("cot") for _ in range(X - 1)]
    cot_sib = sem("cot")
    for i in range(1, X):
        send(cot, cotb.at[head], cot_s[i - 1], cot_r[i - 1], at_x(lax.rem(x + i, X)))
    send(cot, cotb.at[head], cot_s[X - 1], cot_sib, sibling)

    def heads(ref, h):
        return ref[:, h * HDIM : (h + 1) * HDIM]

    def forward(h, q, k, v, bias, shares):
        scores = dot_nt(heads(q, h), heads(k, h)) * scale + bias
        e = jnp.exp(scores - jnp.max(scores, axis=-1, keepdims=True))
        part = e * (1.0 / jnp.sum(e, axis=-1, keepdims=True))
        shares[h] = part
        return dot(part.astype(BF16), heads(v, h)).astype(BF16)

    def backward(h, q, k, v, g, shares):
        share = shares[h]
        weight = share.astype(BF16)
        grad = heads(g, h)
        grad_shares = dot_nt(grad, heads(v, h))
        centre = jnp.sum(share * grad_shares, axis=-1, keepdims=True)
        grad_scores = (share * (grad_shares - centre)).astype(BF16)
        dq = (dot(grad_scores, heads(k, h)) * scale).astype(BF16)
        dk = (dot_tn(grad_scores, heads(q, h)) * scale).astype(BF16)
        dv = dot_tn(weight, grad).astype(BF16)
        return dq, dk, dv

    for (src, dst), l in zip(spatial, spatial_l):
        wait_for(dst, l)
    NB = mask.shape[-1]
    tile = TOK // NB
    rows = lax.broadcasted_iota(jnp.int32, (TOK, TOK), 0)
    cols = lax.broadcasted_iota(jnp.int32, (TOK, TOK), 1)
    for h in range(HL):
        bias = jnp.zeros((TOK, TOK), F32)
        for a in range(NB):
            for b in range(NB):
                value = (mask[0, 0, h, a, b].astype(F32) - 1.0) * -NEG
                inside = jnp.logical_and(rows // tile == a, cols // tile == b)
                bias = jnp.where(inside, value, bias)
        s_att[:, h * HDIM : (h + 1) * HDIM] = forward(h, sq, sk, sv, bias, s_shares)

    def hop_w(j):
        for piece in range(2):
            wz.hop(piece, j)
            wy.hop(piece, j)

    wait_for(own_s, mir_r)
    wz.hop(1, 1)
    wait_for(wtt.at[y, 1], own_l[1])
    wait_for(wtt.at[y, pl.ds(0, Z // 2 - 1)], zq_r[0])
    wy.hop(0, 1)
    wait_for(wtt.at[y, pl.ds(0, Z // 2)], zq_r[1])
    wy.hop(1, 1)
    hop_w(2)

    for (src, dst), r, l in zip(qkv, qkv_r, qkv_l):
        wait_for(rest(dst), r)
        wait_for(dst.at[mine], l)
    same = jnp.where(lax.rem(rows, TB) == lax.rem(cols, TB), 0.0, NEG).astype(F32)
    for h in range(HL):
        t_att_tok[:, h * HDIM : (h + 1) * HDIM] = forward(h, tqb, tkb, tvb, same, t_shares)
    ta_s, ta_r = sem("ta"), sem("ta")
    all_to_all(t_att_tok, t_att, ta_s, ta_r)
    t_att[mine] = t_att_tok[mine]
    hop_w(3)

    fwd_s, fwd_r = [[sem("cot") for _ in range(X - 1)] for _ in range(2)]
    for i in range(1, X):
        slot = cotb.at[lax.rem(x + X - i, X) * 2 + core]
        wait_for(slot, cot_r[i - 1])
        send(slot, slot, fwd_s[i - 1], fwd_r[i - 1], sibling)
    for j in range(4, Z // 2 + 1):
        hop_w(j)
    wait_for(cotb.at[head], cot_l)
    wait_for(cotb.at[head], cot_sib)
    for i in range(1, X):
        wait_for(cotb.at[head], fwd_r[i - 1])
    wait_for(rest(t_att), ta_r)

    @pl.loop(0, Z)
    def _(b):
        both = dot_tn(cotb[b], jnp.concatenate([s_att[...], t_att[...]], axis=1)).astype(BF16)
        ps[b] = both[:, :LW].reshape(Y, Q, LW)
        pt[:, pl.ds(b, 1)] = both[:, LW:].reshape(Y, 1, Q, LW)

    class Scatter(Ring):
        def __init__(self, part, n, me, where, buf, landing):
            super().__init__(part, n, me, where)
            self.buf, self.landing = buf, landing
            size = buf.shape[1] // 2
            self.rows = [pl.ds(0, size), pl.ds(size, size)]

        def landed(self, way, piece, j):
            return self.landing.at[way, j - 1, self.rows[piece]]

        def hop(self, piece, j):
            for way in range(2):
                hops = self.hops(way, piece)
                if j <= hops:
                    dest = self.place(way, hops + 1 - j)
                    if j > 1:
                        came = self.landed(way, piece, j - 1)
                        wait_for(came, self.sems[way, piece][j - 2][1])
                        total = self.buf[dest, self.rows[piece]].astype(F32) + came[...].astype(F32)
                        self.buf[dest, self.rows[piece]] = total.astype(BF16)
                    send(
                        self.buf.at[dest, self.rows[piece]], self.landed(way, piece, j),
                        *self.sems[way, piece][j - 1], self.to[way],
                    )

        def finish(self, piece):
            total = self.buf[self.me, self.rows[piece]].astype(F32)
            for way in range(2):
                hops = self.hops(way, piece)
                came = self.landed(way, piece, hops)
                wait_for(came, self.sems[way, piece][hops - 1][1])
                total = total + came[...].astype(F32)
            self.buf[self.me, self.rows[piece]] = total.astype(BF16)

        def drain(self):
            for (way, piece), pairs in self.sems.items():
                for s, _ in pairs:
                    wait_for(self.buf.at[self.me, self.rows[piece]], s)

    rz = Scatter("p", Z, z, at_z, ps, rs_s)
    ry = Scatter("p", Y, y, at_y, pt, rs_t)

    def hop_p(j):
        for piece in range(2):
            rz.hop(piece, j)
            ry.hop(piece, j)

    hop_p(1)
    wz.finish()
    wy.finish()

    def block_t(b):
        return wtt[:, pl.ds(lax.rem(b - z + 1 + Z, Z), 1)].reshape(DH, LW)

    def block_s(b):
        return wts[b].reshape(DH, LW)

    gt_acc[...] = jnp.zeros_like(gt_acc)

    @pl.loop(0, Z)
    def _(b):
        gt_acc[...] += dot(cotb[b], block_t(b))

    g_t[...] = gt_acc[...].astype(BF16)
    gt_s, gt_r = sem("gt"), sem("gt")
    all_to_all(g_t, g_tok, gt_s, gt_r)
    g_tok[mine] = g_t[mine]
    hop_p(2)

    def update(b):
        return dot_nt(s_att[...], block_s(b)) + dot_nt(t_att[...], block_t(b))

    us_s, us_r = sem("u"), sem("u")

    @pl.loop(0, X)
    def _(i):
        u_out[i] = update(i * 2 + 1 - core).astype(BF16)
        send(u_out.at[i], u_in.at[i], us_s, us_r, sibling)

    gs_acc[...] = jnp.zeros_like(gs_acc)

    @pl.loop(0, Z)
    def _(b):
        gs_acc[...] += dot(cotb[b], block_s(b))

    hop_p(3)

    wait_for(rest(g_tok), gt_r)
    for h in range(HL):
        f = slice(h * HDIM, (h + 1) * HDIM)
        q_g[:, f], k_g[:, f], v_g[:, f] = backward(h, tqb, tkb, tvb, g_tok, t_shares)
    grads = ((q_g, gtq), (k_g, gtk), (v_g, gtv))
    grads_s, grads_r = [[sem("grads") for _ in grads] for _ in range(2)]
    for (src, dst), s, r in zip(grads, grads_s, grads_r):
        all_to_all(src, dst, s, r)
        dst[mine] = src[mine]

    @pl.loop(0, X)
    def _(i):
        u_keep[i] = update(i * 2 + core)

    wait_for(u_in, us_r)
    ux_s, ux_r = sem("u"), sem("u")

    @pl.loop(1, X)
    def _(i):
        other = lax.rem(x + i, X)
        u_send[i - 1] = (u_keep[other] + u_in[other].astype(F32)).astype(BF16)
        send(u_send.at[i - 1], u_recv.at[i - 1], ux_s, ux_r, at_x(other))

    for j in range(4, Z // 2 + 1):
        hop_p(j)

    g_s = gs_acc[...].astype(BF16)
    for h in range(HL):
        f = slice(h * HDIM, (h + 1) * HDIM)
        gsq[:, f], gsk[:, f], gsv[:, f] = backward(h, sq, sk, sv, g_s, s_shares)

    sec_ss, sec_sr, sec_ts, sec_tr = [sem("sec") for _ in range(4)]
    rz.finish(0)
    rz.finish(1)

    @pl.loop(1, Y)
    def _(i):
        other = lax.rem(y + i, Y)
        send(ps.at[z, other], sec_s.at[i - 1], sec_ss, sec_sr, at_y(other))

    ry.finish(0)
    ry.finish(1)

    @pl.loop(1, Z)
    def _(i):
        other = lax.rem(z + i, Z)
        send(pt.at[y, other], sec_t.at[i - 1], sec_ts, sec_tr, at_z(other))

    wait_for(u_recv, ux_r)
    total = u_keep[x] + u_in[x].astype(F32)
    for i in range(X - 1):
        total = total + u_recv[i].astype(F32)
    upd[...] = total.astype(BF16)

    wait_for(sec_s, sec_sr)
    total = ps[z, y].astype(F32)
    for i in range(Y - 1):
        total = total + sec_s[i].astype(F32)
    fin[dp, 0] = (total * (1.0 / NDP)).astype(BF16)
    wait_for(sec_t, sec_tr)
    total = pt[y, z].astype(F32)
    for i in range(Z - 1):
        total = total + sec_t[i].astype(F32)
    fin[dp, 1] = (total * (1.0 / NDP)).astype(BF16)

    fin_s, fin_r = sem("fin"), sem("fin")

    @pl.loop(1, NDP)
    def _(i):
        send(fin.at[dp], fin.at[dp], fin_s, fin_r, {"dp": lax.rem(dp + i, NDP)})

    for (src, dst), r in zip(grads, grads_r):
        wait_for(rest(dst), r)

    for (src, dst), s in zip(qkv, qkv_s):
        wait_for(rest(dst), s)
    wait_for(own_s, mir_s)
    wait_for(wtt.at[y, pl.ds(0, Z - 1)], zq_s)
    for s in cot_s + fwd_s:
        wait_for(cotb.at[head], s)
    wz.drain()
    wy.drain()
    rz.drain()
    ry.drain()
    for s in (ta_s, gt_s):
        wait_for(rest(t_att), s)
    for s in grads_s:
        wait_for(rest(t_att), s)
    wait_for(u_in, us_s)
    wait_for(u_recv, ux_s)
    wait_for(sec_s, sec_ss)
    wait_for(sec_t, sec_ts)
    wait_for(fin.at[pl.ds(0, NDP - 1)], fin_r)
    wait_for(fin.at[pl.ds(0, NDP - 1)], fin_s)
    gsp[...] = fin[:, 0].reshape(DS, LW).astype(F32)
    gtp[...] = fin[:, 1].reshape(DS, LW).astype(F32)


def store(*refs):
    count = len(refs) // 2
    sems = refs[-1]
    copies = [pltpu.make_async_copy(refs[i], refs[count + i], sems.at[i]) for i in range(count)]
    for copy in copies:
        copy.start()
    for copy in copies:
        copy.wait()


def per_device(dims, *args):
    NDP, NSEQ, NHEAD = dims
    sq, sk, sv, mask, tq, tk, tv, sp, tp, cot = args
    tokens, width = sq.shape[2:]
    HL = mask.shape[2]
    HDIM = width // HL
    DS, DH = sp.shape[1], cot.shape[3]
    Z, Y, X = NSEQ // 2, NDP * 2, NHEAD // 2
    Q = DS // NDP
    flat = [a.reshape(a.shape[2:]) for a in (sq, sk, sv, tq, tk, tv, cot)]
    held = flat[:6] + [p.T.reshape(NDP, Q, width) for p in (sp, tp)] + flat[6:]
    mask = pltpu.with_memory_space_constraint(mask, pltpu.HBM)
    held = [pltpu.with_memory_space_constraint(a, pltpu.HBM) for a in held]
    vmem = pl.BlockSpec(memory_space=pltpu.VMEM)
    hbm = pl.BlockSpec(memory_space=pltpu.HBM)
    feat = jax.ShapeDtypeStruct((tokens, width), BF16)
    proj = jax.ShapeDtypeStruct((DS, width), F32)

    def buf(*shape, dtype=BF16):
        return pltpu.VMEM(shape, dtype)

    feats = functools.partial(buf, tokens, width)
    out = pl.pallas_call(
        functools.partial(kernel, (NDP, NSEQ, NHEAD, HL, HDIM, Q)),
        out_shape=[jax.ShapeDtypeStruct((tokens, DH), BF16)] + [feat] * 6 + [proj] * 2,
        in_specs=[hbm] * 3 + [pl.BlockSpec(memory_space=pltpu.SMEM)] + [hbm] * 6,
        out_specs=[vmem] * 9,
        scratch_shapes=[
            feats(), feats(), feats(),
            buf(Z, Y, Q, width),
            buf(Y, Z, Q, width),
            buf(NHEAD, tokens, DH),
            feats(), feats(), feats(),
            buf(HL, tokens, tokens, dtype=F32),
            buf(HL, tokens, tokens, dtype=F32),
            feats(), feats(), feats(),
            feats(dtype=F32), feats(dtype=F32),
            feats(), feats(), feats(), feats(), feats(),
            buf(Z, Y, Q, width),
            buf(Y, Z, Q, width),
            buf(2, Z // 2, Y, Q, width),
            buf(2, Y // 2, Z, Q, width),
            buf(Y - 1, Q, width),
            buf(Z - 1, Q, width),
            buf(NDP, 2, Q, width),
            buf(X, tokens, DH),
            buf(X, tokens, DH),
            buf(X, tokens, DH, dtype=F32),
            buf(X - 1, tokens, DH),
            buf(X - 1, tokens, DH),
            pltpu.SemaphoreType.DMA((SEMS,)),
        ],
        compiler_params=pltpu.CompilerParams(
            collective_id=0, has_side_effects=True, vmem_limit_bytes=24 * 1024 * 1024
        ),
    )(*held[:3], mask, *held[3:])
    out = [pltpu.with_memory_space_constraint(o, pltpu.VMEM) for o in out]
    out = pl.pallas_call(
        store,
        out_shape=[jax.ShapeDtypeStruct(o.shape, o.dtype) for o in out],
        in_specs=[vmem] * 9,
        out_specs=[hbm] * 9,
        scratch_shapes=[pltpu.SemaphoreType.DMA((9,))],
    )(*out)
    return tuple(o[None, None] for o in out[:7]) + (out[7].T, out[8].T)


def solution(mesh):
    tokens = P("dp", "seq", None, "head")
    weights = P("head", "seq")
    dims = tuple(mesh.shape[a] for a in ("dp", "seq", "head"))
    return jax.shard_map(
        functools.partial(per_device, dims),
        mesh=mesh,
        in_specs=(tokens,) * 3 + (P("dp", "seq", "head", None, None),) + (tokens,) * 3 + (weights,) * 2 + (tokens,),
        out_specs=(tokens,) * 7 + (weights,) * 2,
        check_vma=False,
    )
```

time: 119 us -> 96.8 us (0.81)
  local copies, waits for them, and re-layouts: 11.7 us -> 0 us
  Pallas kernels: 106 us -> 95.8 us
    unnamed x27 -> x0, local copies, waits for them, and re-layouts: 11.7 us -> none
    pallas_call x1, Pallas kernels: 106 us -> 94.7 us  [per_device(): pl.pallas_call(functools.partial(kernel, (NDP, NSEQ, NHEAD, HL, HDIM, Q))...]
where the time goes in v2:
time: 96.8 us; the launch traced here: 96.5 us
  Pallas kernels  95.8 us (99%)
    pallas_call x1, Pallas kernels, per_device(): pl.pallas_call(functools.partial(kernel, (NDP, NSEQ, NHEAD, HL, HDIM, Q))...  94.7 us

profile of v2, /device:TPU:56, one launch (start us, length us, event | category | flops | bytes accessed | tf_op | source)
XLA Modules:
  0.0 96.5 jit_solution(10349547242728124164)
XLA Ops:
  0.6 94.7 %shard_map.169 = (bf16[256,384]{1,0:T(8,128)(2,1)S(1)}, bf16[256,256]{1,0:T(8,128)(2,1)S(1)}, bf16[256,256]{1,0:T(8,128)(2,1)S(1)}, bf16[256,256]{1,0:T(8,128)(2...) custom-call(bf16[256,256]{1,0:T(8,128)(2,1)} %bitcast.23, ...), custom_call_target="tpu_custom_call" | custom-call | tf_op jit(solution)/shard_map/pallas_call | solution.py:502
  95.3 1.2 %shard_map.170 = (bf16[256,384]{1,0:T(8,128)(2,1)}, bf16[256,256]{1,0:T(8,128)(2,1)}, bf16[256,256]{1,0:T(8,128)(2,1)}, bf16[256,256]{1,0:T(8,128)(2,1)}, bf16[2...) custom-call(bf16[256,384]{1,0:T(8,128)(2,1)S(1)} %get-tuple-element., ...), custom_call_target="tpu_custom_call" | custom-call | tf_op jit(solution)/shard_map/pallas_call | solution.py:537

commit v3 on v2

--- a/solution.py
+++ b/solution.py
@@ -12,6 +12,10 @@
 BF16 = jnp.bfloat16
 F32 = jnp.float32
 NEG = -1e30
+ORDER = (
+    "sf w1 tf wz2 wy2 c wz3 wy3 cd ps pt rz1 ry1 wz4 wy4 rz2 ry2 rz3 "
+    "ry3 gt wzf u1 rz4 ry4 sa ta tb u2 ss ts gs sb ud"
+).split()
 SEMS = 192
 
 
@@ -113,6 +117,27 @@
 
     pl.semaphore_wait(barrier, NSEQ - 1 + 2 * (NDP - 1) + X)
 
+    def all_to_all(src, dst, send_sem, recv_sem):
+        mine = pl.ds(pl.multiple_of(seq * TB, TB), TB)
+
+        @pl.loop(1, NSEQ)
+        def _(i):
+            other = lax.rem(seq + i, NSEQ)
+            send(
+                src.at[pl.ds(pl.multiple_of(other * TB, TB), TB)], dst.at[mine],
+                send_sem, recv_sem, {"seq": other},
+            )
+
+    def rest(ref):
+        return ref.at[pl.ds(0, (NSEQ - 1) * TB)]
+
+    mine = pl.ds(pl.multiple_of(seq * TB, TB), TB)
+    qkv = ((tq, tqb), (tk, tkb), (tv, tvb))
+    qkv_s, qkv_r, qkv_l = [[sem("qkv") for _ in qkv] for _ in range(3)]
+    for (src, dst), s, r, l in zip(qkv, qkv_s, qkv_r, qkv_l):
+        all_to_all(src, dst, s, r)
+        local(src.at[mine], dst.at[mine], l)
+
     def spatial_piece(chunk, piece):
         return wts.at[chunk, pl.ds((yh if piece == 0 else 1 - yh) * NDP, NDP)]
 
@@ -172,27 +197,6 @@
     wy = Gather("w", Y, y, at_y, temporal_piece)
     wait_for(own_s, own_l[0])
     wz.hop(0, 1)
-
-    def all_to_all(src, dst, send_sem, recv_sem):
-        mine = pl.ds(pl.multiple_of(seq * TB, TB), TB)
-
-        @pl.loop(1, NSEQ)
-        def _(i):
-            other = lax.rem(seq + i, NSEQ)
-            send(
-                src.at[pl.ds(pl.multiple_of(other * TB, TB), TB)], dst.at[mine],
-                send_sem, recv_sem, {"seq": other},
-            )
-
-    def rest(ref):
-        return ref.at[pl.ds(0, (NSEQ - 1) * TB)]
-
-    mine = pl.ds(pl.multiple_of(seq * TB, TB), TB)
-    qkv = ((tq, tqb), (tk, tkb), (tv, tvb))
-    qkv_s, qkv_r, qkv_l = [[sem("qkv") for _ in qkv] for _ in range(3)]
-    for (src, dst), s, r, l in zip(qkv, qkv_s, qkv_r, qkv_l):
-        all_to_all(src, dst, s, r)
-        local(src.at[mine], dst.at[mine], l)
 
     cot_s = [sem("cot") for _ in range(X)]
     cot_r = [sem("cot") for _ in range(X - 1)]
@@ -222,65 +226,6 @@
         dk = (dot_tn(grad_scores, heads(q, h)) * scale).astype(BF16)
         dv = dot_tn(weight, grad).astype(BF16)
         return dq, dk, dv
-
-    for (src, dst), l in zip(spatial, spatial_l):
-        wait_for(dst, l)
-    NB = mask.shape[-1]
-    tile = TOK // NB
-    rows = lax.broadcasted_iota(jnp.int32, (TOK, TOK), 0)
-    cols = lax.broadcasted_iota(jnp.int32, (TOK, TOK), 1)
-    for h in range(HL):
-        bias = jnp.zeros((TOK, TOK), F32)
-        for a in range(NB):
-            for b in range(NB):
-                value = (mask[0, 0, h, a, b].astype(F32) - 1.0) * -NEG
-                inside = jnp.logical_and(rows // tile == a, cols // tile == b)
-                bias = jnp.where(inside, value, bias)
-        s_att[:, h * HDIM : (h + 1) * HDIM] = forward(h, sq, sk, sv, bias, s_shares)
-
-    def hop_w(j):
-        for piece in range(2):
-            wz.hop(piece, j)
-            wy.hop(piece, j)
-
-    wait_for(own_s, mir_r)
-    wz.hop(1, 1)
-    wait_for(wtt.at[y, 1], own_l[1])
-    wait_for(wtt.at[y, pl.ds(0, Z // 2 - 1)], zq_r[0])
-    wy.hop(0, 1)
-    wait_for(wtt.at[y, pl.ds(0, Z // 2)], zq_r[1])
-    wy.hop(1, 1)
-    hop_w(2)
-
-    for (src, dst), r, l in zip(qkv, qkv_r, qkv_l):
-        wait_for(rest(dst), r)
-        wait_for(dst.at[mine], l)
-    same = jnp.where(lax.rem(rows, TB) == lax.rem(cols, TB), 0.0, NEG).astype(F32)
-    for h in range(HL):
-        t_att_tok[:, h * HDIM : (h + 1) * HDIM] = forward(h, tqb, tkb, tvb, same, t_shares)
-    ta_s, ta_r = sem("ta"), sem("ta")
-    all_to_all(t_att_tok, t_att, ta_s, ta_r)
-    t_att[mine] = t_att_tok[mine]
-    hop_w(3)
-
-    fwd_s, fwd_r = [[sem("cot") for _ in range(X - 1)] for _ in range(2)]
-    for i in range(1, X):
-        slot = cotb.at[lax.rem(x + X - i, X) * 2 + core]
-        wait_for(slot, cot_r[i - 1])
-        send(slot, slot, fwd_s[i - 1], fwd_r[i - 1], sibling)
-    for j in range(4, Z // 2 + 1):
-        hop_w(j)
-    wait_for(cotb.at[head], cot_l)
-    wait_for(cotb.at[head], cot_sib)
-    for i in range(1, X):
-        wait_for(cotb.at[head], fwd_r[i - 1])
-    wait_for(rest(t_att), ta_r)
-
-    @pl.loop(0, Z)
-    def _(b):
-        both = dot_tn(cotb[b], jnp.concatenate([s_att[...], t_att[...]], axis=1)).astype(BF16)
-        ps[b] = both[:, :LW].reshape(Y, Q, LW)
-        pt[:, pl.ds(b, 1)] = both[:, LW:].reshape(Y, 1, Q, LW)
 
     class Scatter(Ring):
         def __init__(self, part, n, me, where, buf, landing):
@@ -324,122 +269,191 @@
     rz = Scatter("p", Z, z, at_z, ps, rs_s)
     ry = Scatter("p", Y, y, at_y, pt, rs_t)
 
-    def hop_p(j):
-        for piece in range(2):
-            rz.hop(piece, j)
-            ry.hop(piece, j)
-
-    hop_p(1)
-    wz.finish()
-    wy.finish()
-
     def block_t(b):
         return wtt[:, pl.ds(lax.rem(b - z + 1 + Z, Z), 1)].reshape(DH, LW)
 
     def block_s(b):
         return wts[b].reshape(DH, LW)
 
-    gt_acc[...] = jnp.zeros_like(gt_acc)
-
-    @pl.loop(0, Z)
-    def _(b):
-        gt_acc[...] += dot(cotb[b], block_t(b))
-
-    g_t[...] = gt_acc[...].astype(BF16)
-    gt_s, gt_r = sem("gt"), sem("gt")
-    all_to_all(g_t, g_tok, gt_s, gt_r)
-    g_tok[mine] = g_t[mine]
-    hop_p(2)
-
     def update(b):
         return dot_nt(s_att[...], block_s(b)) + dot_nt(t_att[...], block_t(b))
 
-    us_s, us_r = sem("u"), sem("u")
-
-    @pl.loop(0, X)
-    def _(i):
-        u_out[i] = update(i * 2 + 1 - core).astype(BF16)
-        send(u_out.at[i], u_in.at[i], us_s, us_r, sibling)
-
-    gs_acc[...] = jnp.zeros_like(gs_acc)
-
-    @pl.loop(0, Z)
-    def _(b):
-        gs_acc[...] += dot(cotb[b], block_s(b))
-
-    hop_p(3)
-
-    wait_for(rest(g_tok), gt_r)
-    for h in range(HL):
-        f = slice(h * HDIM, (h + 1) * HDIM)
-        q_g[:, f], k_g[:, f], v_g[:, f] = backward(h, tqb, tkb, tvb, g_tok, t_shares)
+    rows = lax.broadcasted_iota(jnp.int32, (TOK, TOK), 0)
+    cols = lax.broadcasted_iota(jnp.int32, (TOK, TOK), 1)
+    ta_s, ta_r, gt_s, gt_r = sem("ta"), sem("ta"), sem("gt"), sem("gt")
+    fwd_s, fwd_r = [[sem("cot") for _ in range(X - 1)] for _ in range(2)]
+    us_s, us_r, ux_s, ux_r = [sem("u") for _ in range(4)]
     grads = ((q_g, gtq), (k_g, gtk), (v_g, gtv))
     grads_s, grads_r = [[sem("grads") for _ in grads] for _ in range(2)]
-    for (src, dst), s, r in zip(grads, grads_s, grads_r):
-        all_to_all(src, dst, s, r)
-        dst[mine] = src[mine]
-
-    @pl.loop(0, X)
-    def _(i):
-        u_keep[i] = update(i * 2 + core)
-
-    wait_for(u_in, us_r)
-    ux_s, ux_r = sem("u"), sem("u")
-
-    @pl.loop(1, X)
-    def _(i):
-        other = lax.rem(x + i, X)
-        u_send[i - 1] = (u_keep[other] + u_in[other].astype(F32)).astype(BF16)
-        send(u_send.at[i - 1], u_recv.at[i - 1], ux_s, ux_r, at_x(other))
-
-    for j in range(4, Z // 2 + 1):
-        hop_p(j)
-
-    g_s = gs_acc[...].astype(BF16)
-    for h in range(HL):
-        f = slice(h * HDIM, (h + 1) * HDIM)
-        gsq[:, f], gsk[:, f], gsv[:, f] = backward(h, sq, sk, sv, g_s, s_shares)
-
     sec_ss, sec_sr, sec_ts, sec_tr = [sem("sec") for _ in range(4)]
-    rz.finish(0)
-    rz.finish(1)
-
-    @pl.loop(1, Y)
-    def _(i):
-        other = lax.rem(y + i, Y)
-        send(ps.at[z, other], sec_s.at[i - 1], sec_ss, sec_sr, at_y(other))
-
-    ry.finish(0)
-    ry.finish(1)
-
-    @pl.loop(1, Z)
-    def _(i):
-        other = lax.rem(z + i, Z)
-        send(pt.at[y, other], sec_t.at[i - 1], sec_ts, sec_tr, at_z(other))
-
-    wait_for(u_recv, ux_r)
-    total = u_keep[x] + u_in[x].astype(F32)
-    for i in range(X - 1):
-        total = total + u_recv[i].astype(F32)
-    upd[...] = total.astype(BF16)
-
-    wait_for(sec_s, sec_sr)
-    total = ps[z, y].astype(F32)
-    for i in range(Y - 1):
-        total = total + sec_s[i].astype(F32)
-    fin[dp, 0] = (total * (1.0 / NDP)).astype(BF16)
-    wait_for(sec_t, sec_tr)
-    total = pt[y, z].astype(F32)
-    for i in range(Z - 1):
-        total = total + sec_t[i].astype(F32)
-    fin[dp, 1] = (total * (1.0 / NDP)).astype(BF16)
-
-    fin_s, fin_r = sem("fin"), sem("fin")
-
-    @pl.loop(1, NDP)
-    def _(i):
-        send(fin.at[dp], fin.at[dp], fin_s, fin_r, {"dp": lax.rem(dp + i, NDP)})
-
+    fin_ss, fin_sr, fin_ts, fin_tr = [sem("fin") for _ in range(4)]
+
+    def spatial_forward():
+        for (src, dst), l in zip(spatial, spatial_l):
+            wait_for(dst, l)
+        NB = mask.shape[-1]
+        tile = TOK // NB
+        for h in range(HL):
+            bias = jnp.zeros((TOK, TOK), F32)
+            for a in range(NB):
+                for b in range(NB):
+                    value = (mask[0, 0, h, a, b].astype(F32) - 1.0) * -NEG
+                    inside = jnp.logical_and(rows // tile == a, cols // tile == b)
+                    bias = jnp.where(inside, value, bias)
+            s_att[:, h * HDIM : (h + 1) * HDIM] = forward(h, sq, sk, sv, bias, s_shares)
+
+    def weights_start():
+        wait_for(own_s, mir_r)
+        wz.hop(1, 1)
+        wait_for(wtt.at[y, 1], own_l[1])
+        wait_for(wtt.at[y, pl.ds(0, Z // 2 - 1)], zq_r[0])
+        wy.hop(0, 1)
+        wait_for(wtt.at[y, pl.ds(0, Z // 2)], zq_r[1])
+        wy.hop(1, 1)
+
+    def temporal_forward():
+        for (src, dst), r, l in zip(qkv, qkv_r, qkv_l):
+            wait_for(rest(dst), r)
+            wait_for(dst.at[mine], l)
+        same = jnp.where(lax.rem(rows, TB) == lax.rem(cols, TB), 0.0, NEG).astype(F32)
+        for h in range(HL):
+            t_att_tok[:, h * HDIM : (h + 1) * HDIM] = forward(h, tqb, tkb, tvb, same, t_shares)
+        all_to_all(t_att_tok, t_att, ta_s, ta_r)
+        t_att[mine] = t_att_tok[mine]
+
+    def cotangent_on():
+        for i in range(1, X):
+            slot = cotb.at[lax.rem(x + X - i, X) * 2 + core]
+            wait_for(slot, cot_r[i - 1])
+            send(slot, slot, fwd_s[i - 1], fwd_r[i - 1], sibling)
+
+    def cotangent_done():
+        wait_for(cotb.at[head], cot_l)
+        wait_for(cotb.at[head], cot_sib)
+        for i in range(1, X):
+            wait_for(cotb.at[head], fwd_r[i - 1])
+
+    def spatial_product():
+        @pl.loop(0, Z)
+        def _(b):
+            ps[b] = dot_tn(cotb[b], s_att[...]).astype(BF16).reshape(Y, Q, LW)
+
+    def temporal_product():
+        wait_for(rest(t_att), ta_r)
+
+        @pl.loop(0, Z)
+        def _(b):
+            pt[:, pl.ds(b, 1)] = dot_tn(cotb[b], t_att[...]).astype(BF16).reshape(Y, 1, Q, LW)
+
+    def temporal_gradient():
+        wy.finish()
+        gt_acc[...] = jnp.zeros_like(gt_acc)
+
+        @pl.loop(0, Z)
+        def _(b):
+            gt_acc[...] += dot(cotb[b], block_t(b))
+
+        g_t[...] = gt_acc[...].astype(BF16)
+        all_to_all(g_t, g_tok, gt_s, gt_r)
+        g_tok[mine] = g_t[mine]
+
+    def spatial_gradient():
+        gs_acc[...] = jnp.zeros_like(gs_acc)
+
+        @pl.loop(0, Z)
+        def _(b):
+            gs_acc[...] += dot(cotb[b], block_s(b))
+
+    def update_other():
+        @pl.loop(0, X)
+        def _(i):
+            u_out[i] = update(i * 2 + 1 - core).astype(BF16)
+            send(u_out.at[i], u_in.at[i], us_s, us_r, sibling)
+
+    def update_own():
+        @pl.loop(0, X)
+        def _(i):
+            u_keep[i] = update(i * 2 + core)
+
+        wait_for(u_in, us_r)
+
+        @pl.loop(1, X)
+        def _(i):
+            other = lax.rem(x + i, X)
+            u_send[i - 1] = (u_keep[other] + u_in[other].astype(F32)).astype(BF16)
+            send(u_send.at[i - 1], u_recv.at[i - 1], ux_s, ux_r, at_x(other))
+
+    def update_done():
+        wait_for(u_recv, ux_r)
+        total = u_keep[x] + u_in[x].astype(F32)
+        for i in range(X - 1):
+            total = total + u_recv[i].astype(F32)
+        upd[...] = total.astype(BF16)
+
+    def temporal_backward():
+        wait_for(rest(g_tok), gt_r)
+        for h in range(HL):
+            f = slice(h * HDIM, (h + 1) * HDIM)
+            q_g[:, f], k_g[:, f], v_g[:, f] = backward(h, tqb, tkb, tvb, g_tok, t_shares)
+        for (src, dst), s, r in zip(grads, grads_s, grads_r):
+            all_to_all(src, dst, s, r)
+            dst[mine] = src[mine]
+
+    def spatial_backward():
+        g_s = gs_acc[...].astype(BF16)
+        for h in range(HL):
+            f = slice(h * HDIM, (h + 1) * HDIM)
+            gsq[:, f], gsk[:, f], gsv[:, f] = backward(h, sq, sk, sv, g_s, s_shares)
+
+    def spatial_across():
+        rz.finish(0)
+        rz.finish(1)
+
+        @pl.loop(1, Y)
+        def _(i):
+            other = lax.rem(y + i, Y)
+            send(ps.at[z, other], sec_s.at[i - 1], sec_ss, sec_sr, at_y(other))
+
+    def temporal_across():
+        ry.finish(0)
+        ry.finish(1)
+
+        @pl.loop(1, Z)
+        def _(i):
+            other = lax.rem(z + i, Z)
+            send(pt.at[y, other], sec_t.at[i - 1], sec_ts, sec_tr, at_z(other))
+
+    def share(own, parts, count, slot, left, came):
+        total = own.astype(F32)
+        for i in range(count - 1):
+            total = total + parts[i].astype(F32)
+        fin[slot, dp] = (total * (1.0 / NDP)).astype(BF16)
+
+        @pl.loop(1, NDP)
+        def _(i):
+            send(fin.at[slot, dp], fin.at[slot, dp], left, came, {"dp": lax.rem(dp + i, NDP)})
+
+    def spatial_share():
+        wait_for(sec_s, sec_sr)
+        share(ps[z, y], sec_s, Y, 0, fin_ss, fin_sr)
+
+    def temporal_share():
+        wait_for(sec_t, sec_tr)
+        share(pt[y, z], sec_t, Z, 1, fin_ts, fin_tr)
+
+    steps = {
+        "sf": spatial_forward, "w1": weights_start, "tf": temporal_forward, "c": cotangent_on, "cd": cotangent_done,
+        "ps": spatial_product, "pt": temporal_product, "gt": temporal_gradient, "gs": spatial_gradient,
+        "wzf": wz.finish, "u1": update_other, "u2": update_own, "ud": update_done, "tb": temporal_backward,
+        "sb": spatial_backward, "sa": spatial_across, "ta": temporal_across, "ss": spatial_share, "ts": temporal_share,
+    }
+    rings = {"wz": wz, "wy": wy, "rz": rz, "ry": ry}
+    for name in ORDER:
+        if name in steps:
+            steps[name]()
+        else:
+            for piece in range(2):
+                rings[name[:2]].hop(piece, int(name[2:]))
     for (src, dst), r in zip(grads, grads_r):
         wait_for(rest(dst), r)
 
@@ -461,10 +475,10 @@
     wait_for(u_recv, ux_s)
     wait_for(sec_s, sec_ss)
     wait_for(sec_t, sec_ts)
-    wait_for(fin.at[pl.ds(0, NDP - 1)], fin_r)
-    wait_for(fin.at[pl.ds(0, NDP - 1)], fin_s)
-    gsp[...] = fin[:, 0].reshape(DS, LW).astype(F32)
-    gtp[...] = fin[:, 1].reshape(DS, LW).astype(F32)
+    for slot, left, came, out in ((0, fin_ss, fin_sr, gsp), (1, fin_ts, fin_tr, gtp)):
+        wait_for(fin.at[slot, pl.ds(0, NDP - 1)], came)
+        wait_for(fin.at[slot, pl.ds(0, NDP - 1)], left)
+        out[...] = fin[slot].reshape(DS, LW).astype(F32)
 
 
 def store(*refs):
@@ -521,7 +535,7 @@
             buf(2, Y // 2, Z, Q, width),
             buf(Y - 1, Q, width),
             buf(Z - 1, Q, width),
-            buf(NDP, 2, Q, width),
+            buf(2, NDP, Q, width),
             buf(X, tokens, DH),
             buf(X, tokens, DH),
             buf(X, tokens, DH, dtype=F32),

time: 96.8 us -> 95.1 us (0.982)
  the two profiles are of different devices: /device:TPU:56 before, /device:TPU:12 now
where the time goes in v3:
time: 95.1 us; the launch traced here: 94.9 us
  Pallas kernels  94.3 us (99%)
    pallas_call x1, Pallas kernels, per_device(): pl.pallas_call(functools.partial(kernel, (NDP, NSEQ, NHEAD, HL, HDIM, Q))...  93.1 us

profile of v3, /device:TPU:12, one launch (start us, length us, event | category | flops | bytes accessed | tf_op | source)
XLA Modules:
  0.0 94.9 jit_solution(11260764987443918018)
XLA Ops:
  0.6 93.1 %shard_map.169 = (bf16[256,384]{1,0:T(8,128)(2,1)S(1)}, bf16[256,256]{1,0:T(8,128)(2,1)S(1)}, bf16[256,256]{1,0:T(8,128)(2,1)S(1)}, bf16[256,256]{1,0:T(8,128)(2...) custom-call(bf16[256,256]{1,0:T(8,128)(2,1)} %bitcast.23, ...), custom_call_target="tpu_custom_call" | custom-call | tf_op jit(solution)/shard_map/pallas_call | solution.py:516
  93.8 1.2 %shard_map.170 = (bf16[256,384]{1,0:T(8,128)(2,1)}, bf16[256,256]{1,0:T(8,128)(2,1)}, bf16[256,256]{1,0:T(8,128)(2,1)}, bf16[256,256]{1,0:T(8,128)(2,1)}, bf16[2...) custom-call(bf16[256,384]{1,0:T(8,128)(2,1)S(1)} %get-tuple-element., ...), custom_call_target="tpu_custom_call" | custom-call | tf_op jit(solution)/shard_map/pallas_call | solution.py:551

commit v4 on v3

--- a/solution.py
+++ b/solution.py
@@ -13,9 +13,9 @@
 F32 = jnp.float32
 NEG = -1e30
 ORDER = (
-    "sf w1 tf wz2 wy2 c wz3 wy3 cd ps pt rz1 ry1 wz4 wy4 rz2 ry2 rz3 "
-    "ry3 gt wzf u1 rz4 ry4 sa ta tb u2 ss ts gs sb ud"
-).split()
+    "sf", "w1", "tf", "wz2", "wy2", "c", "wz3", "wy3", "cd", "ps", "pt", "rz1", "ry1", "wz4", "wy4", "rz2", "ry2",
+    "rz3", "ry3", "gt", "wzf", "u1", "rz4", "ry4", "sa", "ta", "tb", "u2", "ss", "ts", "gs", "sb", "ud",
+)
 SEMS = 192
 
 
@@ -405,23 +405,22 @@
             f = slice(h * HDIM, (h + 1) * HDIM)
             gsq[:, f], gsk[:, f], gsv[:, f] = backward(h, sq, sk, sv, g_s, s_shares)
 
+    def across(ring, buf, mine, me, n, landing, left, came, where):
+        for piece in range(2):
+            ring.finish(piece)
+
+            @pl.loop(piece * (n // 2), (piece + 1) * (n // 2))
+            def _(other):
+                @pl.when(other != me)
+                def _():
+                    slot = lax.rem(other - me + n, n) - 1
+                    send(buf.at[mine, other], landing.at[slot], left, came, where(other))
+
     def spatial_across():
-        rz.finish(0)
-        rz.finish(1)
-
-        @pl.loop(1, Y)
-        def _(i):
-            other = lax.rem(y + i, Y)
-            send(ps.at[z, other], sec_s.at[i - 1], sec_ss, sec_sr, at_y(other))
+        across(rz, ps, z, y, Y, sec_s, sec_ss, sec_sr, at_y)
 
     def temporal_across():
-        ry.finish(0)
-        ry.finish(1)
-
-        @pl.loop(1, Z)
-        def _(i):
-            other = lax.rem(z + i, Z)
-            send(pt.at[y, other], sec_t.at[i - 1], sec_ts, sec_tr, at_z(other))
+        across(ry, pt, y, z, Z, sec_t, sec_ts, sec_tr, at_z)
 
     def share(own, parts, count, slot, left, came):
         total = own.astype(F32)

time: 95.1 us -> 94.8 us (level)
  the two profiles are of different devices: /device:TPU:12 before, /device:TPU:56 now
where the time goes in v4:
time: 94.8 us; the launch traced here: 94.6 us
  Pallas kernels  94 us (99%)
    pallas_call x1, Pallas kernels, per_device(): pl.pallas_call(functools.partial(kernel, (NDP, NSEQ, NHEAD, HL, HDIM, Q))...  92.8 us

profile of v4, /device:TPU:56, one launch (start us, length us, event | category | flops | bytes accessed | tf_op | source)
XLA Modules:
  0.0 94.6 jit_solution(6085480072441441658)
XLA Ops:
  0.6 92.8 %shard_map.169 = (bf16[256,384]{1,0:T(8,128)(2,1)S(1)}, bf16[256,256]{1,0:T(8,128)(2,1)S(1)}, bf16[256,256]{1,0:T(8,128)(2,1)S(1)}, bf16[256,256]{1,0:T(8,128)(2...) custom-call(bf16[256,256]{1,0:T(8,128)(2,1)} %bitcast.23, ...), custom_call_target="tpu_custom_call" | custom-call | tf_op jit(solution)/shard_map/pallas_call | solution.py:515
  93.5 1.2 %shard_map.170 = (bf16[256,384]{1,0:T(8,128)(2,1)}, bf16[256,256]{1,0:T(8,128)(2,1)}, bf16[256,256]{1,0:T(8,128)(2,1)}, bf16[256,256]{1,0:T(8,128)(2,1)}, bf16[2...) custom-call(bf16[256,384]{1,0:T(8,128)(2,1)S(1)} %get-tuple-element., ...), custom_call_target="tpu_custom_call" | custom-call | tf_op jit(solution)/shard_map/pallas_call | solution.py:550

commit v5 on v4

--- a/solution.py
+++ b/solution.py
@@ -13,7 +13,7 @@
 F32 = jnp.float32
 NEG = -1e30
 ORDER = (
-    "sf", "w1", "tf", "wz2", "wy2", "c", "wz3", "wy3", "cd", "ps", "pt", "rz1", "ry1", "wz4", "wy4", "rz2", "ry2",
+    "w1", "sf", "tf", "wz2", "wy2", "c", "wz3", "wy3", "cd", "ps", "pt", "rz1", "ry1", "wz4", "wy4", "rz2", "ry2",
     "rz3", "ry3", "gt", "wzf", "u1", "rz4", "ry4", "sa", "ta", "tb", "u2", "ss", "ts", "gs", "sb", "ud",
 )
 SEMS = 192

time: 94.8 us -> 93.9 us (level)
  Pallas kernels: 94 us -> 92.7 us
    pallas_call x1, Pallas kernels: 92.8 us -> 91.6 us  [per_device(): pl.pallas_call(functools.partial(kernel, (NDP, NSEQ, NHEAD, HL, HDIM, Q))...]
where the time goes in v5:
time: 93.9 us; the launch traced here: 93.4 us
  Pallas kernels  92.7 us (99%)
    pallas_call x1, Pallas kernels, per_device(): pl.pallas_call(functools.partial(kernel, (NDP, NSEQ, NHEAD, HL, HDIM, Q))...  91.6 us

profile of v5, /device:TPU:56, one launch (start us, length us, event | category | flops | bytes accessed | tf_op | source)
XLA Modules:
  0.0 93.4 jit_solution(9691261333147380879)
XLA Ops:
  0.6 91.6 %shard_map.169 = (bf16[256,384]{1,0:T(8,128)(2,1)S(1)}, bf16[256,256]{1,0:T(8,128)(2,1)S(1)}, bf16[256,256]{1,0:T(8,128)(2,1)S(1)}, bf16[256,256]{1,0:T(8,128)(2...) custom-call(bf16[256,256]{1,0:T(8,128)(2,1)} %bitcast.23, ...), custom_call_target="tpu_custom_call" | custom-call | tf_op jit(solution)/shard_map/pallas_call | solution.py:515
  92.2 1.2 %shard_map.170 = (bf16[256,384]{1,0:T(8,128)(2,1)}, bf16[256,256]{1,0:T(8,128)(2,1)}, bf16[256,256]{1,0:T(8,128)(2,1)}, bf16[256,256]{1,0:T(8,128)(2,1)}, bf16[2...) custom-call(bf16[256,384]{1,0:T(8,128)(2,1)S(1)} %get-tuple-element., ...), custom_call_target="tpu_custom_call" | custom-call | tf_op jit(solution)/shard_map/pallas_call | solution.py:550
